TPU v7x, 128 devices: a whole 4x4x4 slice. The times are simulated.
128 devices in a mesh: dp: 32 (over z, y_hi, x), tensor: 4 (over y_lo, core).
Axes of the slice: x: 4, y: 4 (y_hi: 2, y_lo: 2; y = y_hi * 2 + y_lo), z: 4, core: 2. Of those that a mesh axis runs over, the one named last changes fastest.
Arguments:
- tokens: bfloat16 [16384, 1024], P(('dp', 'tensor')), may hold values from -6 to 6
- cotangent: bfloat16 [16384, 1024], P(('dp', 'tensor')), may hold values from -6 to 6
- lengths: int32 [32, 4], P('dp'), may hold values from 1 to 509, as said below
- small: float32 [5, 1024], P(None, ('dp', 'tensor')), may hold values from -1.5 to 1.5
- mix_in: float32 [3, 1024, 1024], P(None, 'dp', 'tensor'), may hold values from -0.1875 to 0.1875
- mix_out: float32 [1024, 1024], P('dp', 'tensor'), may hold values from -0.1875 to 0.1875
- ffn_gate_up: float32 [2, 1024, 4608], P(None, 'dp', 'tensor'), may hold values from -0.1875 to 0.1875
- ffn_down: float32 [1024, 4608], P('dp', 'tensor'), may hold values from -0.09375 to 0.09375
- small_first: float32 [5, 1024], P(None, ('dp', 'tensor'))
- small_second: float32 [5, 1024], P(None, ('dp', 'tensor'))
- in_first: float32 [3, 1024, 1024], P(None, 'dp', 'tensor')
- in_second: float32 [3, 1024, 1024], P(None, 'dp', 'tensor')
- out_first: float32 [1024, 1024], P('dp', 'tensor')
- out_second: float32 [1024, 1024], P('dp', 'tensor')
- gate_up_first: float32 [2, 1024, 4608], P(None, 'dp', 'tensor')
- gate_up_second: float32 [2, 1024, 4608], P(None, 'dp', 'tensor')
- down_first: float32 [1024, 4608], P('dp', 'tensor')
- down_second: float32 [1024, 4608], P('dp', 'tensor')
Outputs:
- block_out: bfloat16 [16384, 1024], P(('dp', 'tensor'))
- tokens_grad: float32 [16384, 1024], P(('dp', 'tensor'))
- small_moment: float32 [5, 1024], P(None, ('dp', 'tensor'))
- small_square: float32 [5, 1024], P(None, ('dp', 'tensor'))
- small_new: float32 [5, 1024], P(None, ('dp', 'tensor'))
- in_moment: float32 [3, 1024, 1024], P(None, 'dp', 'tensor')
- in_square: float32 [3, 1024, 1024], P(None, 'dp', 'tensor')
- in_new: float32 [3, 1024, 1024], P(None, 'dp', 'tensor')
- out_moment: float32 [1024, 1024], P('dp', 'tensor')
- out_square: float32 [1024, 1024], P('dp', 'tensor')
- out_new: float32 [1024, 1024], P('dp', 'tensor')
- gate_up_moment: float32 [2, 1024, 4608], P(None, 'dp', 'tensor')
- gate_up_square: float32 [2, 1024, 4608], P(None, 'dp', 'tensor')
- gate_up_new: float32 [2, 1024, 4608], P(None, 'dp', 'tensor')
- down_moment: float32 [1024, 4608], P('dp', 'tensor')
- down_square: float32 [1024, 4608], P('dp', 'tensor')
- down_new: float32 [1024, 4608], P('dp', 'tensor')
Inputs may be any that keep to these rules, and one draw needn't show every extreme that they name: The lengths of a group sum to at most 512; in every group one sequence covers rows from the first quarter to the last quarter of the group.
All inputs are finite; a program needn't handle non-finite values.
Results may differ from a plain program's by a relative error of at most 0.04.
Values may be sent and summed in bfloat16 or wider, within the bound.
A program may use at most 128 MiB of HBM per device.

v0:
```python
import jax
import jax.numpy as jnp
from jax import lax
from jax.sharding import PartitionSpec as P

STEP = 10


NORM_EPSILON = 1e-05
BETA_FIRST = 0.9
BETA_SECOND = 0.95
ADAM_EPSILON = 1e-08
DECAY_RATE = 0.1
RATE_PROJ = 0.1
RATE_DOWN = 0.045
RATE_SMALL = 0.6


def seq_layout(lens, rows):
    offsets = jnp.cumsum(lens) - lens
    total = jnp.sum(lens)
    starts = jnp.concatenate([offsets, total[None]])
    places = jnp.arange(rows, dtype=jnp.int32)
    before = starts[None, :] <= places[:, None]
    seg_start = jnp.max(jnp.where(before, starts[None, :], 0), axis=1)
    return (places - seg_start, places < total)


def shift_down(values, steps):
    return jnp.pad(values[:-steps], ((steps, 0), (0, 0)))


def shift_up(values, steps):
    return jnp.pad(values[steps:], ((0, steps), (0, 0)))


def adam_step(weight, grad, first, second, rate):
    first_new = BETA_FIRST * first + (1.0 - BETA_FIRST) * grad
    second_new = BETA_SECOND * second + (1.0 - BETA_SECOND) * grad * grad
    first_hat = first_new / (1.0 - BETA_FIRST**STEP)
    second_hat = second_new / (1.0 - BETA_SECOND**STEP)
    weight_new = weight - rate * (
        first_hat / (jnp.sqrt(second_hat) + ADAM_EPSILON) + DECAY_RATE * weight
    )
    return (first_new, second_new, weight_new)


def norm_back(grad_normed, unit, inverse, gain):
    scaled = grad_normed * gain
    gain_grad = jnp.sum(grad_normed * unit, axis=0)
    inner = jnp.mean(scaled * unit, axis=1, keepdims=True)
    return (inverse * (scaled - unit * inner), gain_grad)


def per_device(
    tokens,
    cotangent,
    lengths,
    small,
    mix_in,
    mix_out,
    ffn_gate_up,
    ffn_down,
    small_first,
    small_second,
    in_first,
    in_second,
    out_first,
    out_second,
    gate_up_first,
    gate_up_second,
    down_first,
    down_second,
):
    tensor_count = lax.axis_size("tensor")
    tensor_rank = lax.axis_index("tensor")
    rows_dev = tokens.shape[0]
    width = tokens.shape[1]
    channels = mix_in.shape[2]
    group_rows = rows_dev * tensor_count
    distance, live_all = seq_layout(lengths[0], group_rows)
    live_mine = lax.dynamic_slice_in_dim(live_all, tensor_rank * rows_dev, rows_dev)
    one_tap = (distance >= 1)[:, None].astype(jnp.float32)
    two_tap = (distance >= 2)[:, None].astype(jnp.float32)
    small_all = lax.all_gather(small, ("dp", "tensor"), axis=1, tiled=True)
    gain_one = small_all[0]
    gain_two = small_all[1]
    taps = lax.dynamic_slice_in_dim(small_all[2:5], tensor_rank * channels, channels, 1)
    in_w, out_w, gu_w, down_w = (
        lax.all_gather(mix_in.astype(jnp.bfloat16), "dp", axis=1, tiled=True),
        lax.all_gather(mix_out.astype(jnp.bfloat16), "dp", axis=0, tiled=True),
        lax.all_gather(ffn_gate_up.astype(jnp.bfloat16), "dp", axis=1, tiled=True),
        lax.all_gather(ffn_down.astype(jnp.bfloat16), "dp", axis=0, tiled=True),
    )
    resid = tokens.astype(jnp.float32)
    inv_one = lax.rsqrt(jnp.mean(resid * resid, axis=1, keepdims=True) + NORM_EPSILON)
    unit_one = resid * inv_one
    rows_one = lax.all_gather(
        (unit_one * gain_one).astype(jnp.bfloat16), "tensor", axis=0, tiled=True
    )
    proj = jnp.einsum("rd,jdc->jrc", rows_one, in_w, preferred_element_type=jnp.float32)
    gate_b = proj[0]
    gate_c = proj[1]
    values = proj[2]
    mixed = gate_b * values
    before_one = shift_down(mixed, 1) * one_tap
    before_two = shift_down(mixed, 2) * two_tap
    conv_out = taps[0] * mixed + taps[1] * before_one + taps[2] * before_two
    gated = (gate_c * conv_out).astype(jnp.bfloat16)
    part_rows = gated
    mid = resid + lax.psum_scatter(
        jnp.einsum("rc,dc->rd", part_rows, out_w, preferred_element_type=jnp.float32),
        "tensor",
        scatter_dimension=0,
        tiled=True,
    )
    inv_two = lax.rsqrt(jnp.mean(mid * mid, axis=1, keepdims=True) + NORM_EPSILON)
    unit_two = mid * inv_two
    rows_two = lax.all_gather(
        (unit_two * gain_two).astype(jnp.bfloat16), "tensor", axis=0, tiled=True
    )
    gate_up = jnp.einsum("rd,jdf->jrf", rows_two, gu_w, preferred_element_type=jnp.float32)
    gate_pre = gate_up[0]
    up_val = gate_up[1]
    sigmoid_val = jax.nn.sigmoid(gate_pre)
    silu_val = gate_pre * sigmoid_val
    hidden = (silu_val * up_val).astype(jnp.bfloat16)
    part_rows = hidden
    block_out = (
        mid
        + lax.psum_scatter(
            jnp.einsum("rf,df->rd", part_rows, down_w, preferred_element_type=jnp.float32).astype(
                jnp.bfloat16
            ),
            "tensor",
            scatter_dimension=0,
            tiled=True,
        ).astype(jnp.float32)
    ).astype(jnp.bfloat16)
    grad_out = cotangent * live_mine[:, None].astype(jnp.bfloat16)
    rows_grad = lax.all_gather(grad_out, "tensor", axis=0, tiled=True)
    grad_hidden = jnp.dot(rows_grad, down_w, preferred_element_type=jnp.float32)
    down_grad = jnp.einsum("rd,rf->df", rows_grad, hidden, preferred_element_type=jnp.float32)
    grad_gate = grad_hidden * up_val * sigmoid_val * (1.0 + gate_pre * (1.0 - sigmoid_val))
    grad_up = grad_hidden * silu_val
    grad_gu = jnp.stack([grad_gate, grad_up]).astype(jnp.bfloat16)
    gate_up_grad = jnp.einsum("rd,jrf->jdf", rows_two, grad_gu, preferred_element_type=jnp.float32)
    part_rows = grad_gu
    grad_norm_two = lax.psum_scatter(
        jnp.einsum("jrf,jdf->rd", part_rows, gu_w, preferred_element_type=jnp.float32).astype(
            jnp.bfloat16
        ),
        "tensor",
        scatter_dimension=0,
        tiled=True,
    ).astype(jnp.float32)
    back_two, gain_two_grad = norm_back(grad_norm_two, unit_two, inv_two, gain_two)
    grad_mid = grad_out.astype(jnp.float32) + back_two
    rows_mid = lax.all_gather(grad_mid.astype(jnp.bfloat16), "tensor", axis=0, tiled=True)
    out_grad = jnp.einsum("rd,rc->dc", rows_mid, gated, preferred_element_type=jnp.float32)
    grad_gated = jnp.dot(rows_mid, out_w, preferred_element_type=jnp.float32)
    grad_c = grad_gated * conv_out
    grad_conv = grad_gated * gate_c
    tap_grad = jnp.stack(
        [
            jnp.sum(grad_conv * mixed, axis=0),
            jnp.sum(grad_conv * before_one, axis=0),
            jnp.sum(grad_conv * before_two, axis=0),
        ]
    )
    grad_mixed = (
        taps[0] * grad_conv
        + taps[1] * shift_up(grad_conv * one_tap, 1)
        + taps[2] * shift_up(grad_conv * two_tap, 2)
    )
    grad_proj = jnp.stack([grad_mixed * values, grad_c, grad_mixed * gate_b]).astype(jnp.bfloat16)
    in_grad = jnp.einsum("rd,jrc->jdc", rows_one, grad_proj, preferred_element_type=jnp.float32)
    part_rows = grad_proj
    grad_norm_one = lax.psum_scatter(
        jnp.einsum("jrc,jdc->rd", part_rows, in_w, preferred_element_type=jnp.float32).astype(
            jnp.bfloat16
        ),
        "tensor",
        scatter_dimension=0,
        tiled=True,
    ).astype(jnp.float32)
    back_one, gain_one_grad = norm_back(grad_norm_one, unit_one, inv_one, gain_one)
    tokens_grad = grad_mid + back_one
    tap_full = lax.dynamic_update_slice_in_dim(
        jnp.zeros((3, width), jnp.float32), tap_grad, tensor_rank * channels, 1
    )
    small_terms = jnp.concatenate([gain_one_grad[None], gain_two_grad[None], tap_full], axis=0)
    small_sum = lax.psum_scatter(small_terms, ("dp", "tensor"), scatter_dimension=1, tiled=True)
    in_sum, out_sum, gate_up_sum, down_sum = (
        lax.psum_scatter(
            in_grad.astype(jnp.bfloat16), "dp", scatter_dimension=1, tiled=True
        ).astype(jnp.float32),
        lax.psum_scatter(
            out_grad.astype(jnp.bfloat16), "dp", scatter_dimension=0, tiled=True
        ).astype(jnp.float32),
        lax.psum_scatter(
            gate_up_grad.astype(jnp.bfloat16), "dp", scatter_dimension=1, tiled=True
        ).astype(jnp.float32),
        lax.psum_scatter(
            down_grad.astype(jnp.bfloat16), "dp", scatter_dimension=0, tiled=True
        ).astype(jnp.float32),
    )
    small_moment, small_square, small_new = adam_step(
        small, small_sum, small_first, small_second, RATE_SMALL
    )
    in_moment, in_square, in_new = adam_step(mix_in, in_sum, in_first, in_second, RATE_PROJ)
    out_moment, out_square, out_new = adam_step(mix_out, out_sum, out_first, out_second, RATE_PROJ)
    gate_up_moment, gate_up_square, gate_up_new = adam_step(
        ffn_gate_up, gate_up_sum, gate_up_first, gate_up_second, RATE_PROJ
    )
    down_moment, down_square, down_new = adam_step(
        ffn_down, down_sum, down_first, down_second, RATE_DOWN
    )
    return (
        block_out,
        tokens_grad,
        small_moment,
        small_square,
        small_new,
        in_moment,
        in_square,
        in_new,
        out_moment,
        out_square,
        out_new,
        gate_up_moment,
        gate_up_square,
        gate_up_new,
        down_moment,
        down_square,
        down_new,
    )


def solution(mesh):
    in_specs = (
        P(("dp", "tensor"), None),
        P(("dp", "tensor"), None),
        P("dp", None),
        P(None, ("dp", "tensor")),
        P(None, "dp", "tensor"),
        P("dp", "tensor"),
        P(None, "dp", "tensor"),
        P("dp", "tensor"),
        P(None, ("dp", "tensor")),
        P(None, ("dp", "tensor")),
        P(None, "dp", "tensor"),
        P(None, "dp", "tensor"),
        P("dp", "tensor"),
        P("dp", "tensor"),
        P(None, "dp", "tensor"),
        P(None, "dp", "tensor"),
        P("dp", "tensor"),
        P("dp", "tensor"),
    )
    out_specs = (
        P(("dp", "tensor"), None),
        P(("dp", "tensor"), None),
        P(None, ("dp", "tensor")),
        P(None, ("dp", "tensor")),
        P(None, ("dp", "tensor")),
        P(None, "dp", "tensor"),
        P(None, "dp", "tensor"),
        P(None, "dp", "tensor"),
        P("dp", "tensor"),
        P("dp", "tensor"),
        P("dp", "tensor"),
        P(None, "dp", "tensor"),
        P(None, "dp", "tensor"),
        P(None, "dp", "tensor"),
        P("dp", "tensor"),
        P("dp", "tensor"),
        P("dp", "tensor"),
    )
    return jax.shard_map(
        per_device, mesh=mesh, in_specs=in_specs, out_specs=out_specs, check_vma=False
    )
```

profile of v0, /device:TPU:0, one launch (start us, length us, event | category | flops | bytes accessed | tf_op | source)
XLA Modules:
  0.0 1432.1 jit_solution(11414691803806881457)
XLA Ops:
  7.3 0.8 copy.108
  8.0 180.2 %all_gather.27 = f32[5,1024]{0,1:T(8,128)S(1)} all-gather(f32[5,8]{0,1:T(8,128)S(1)} %copy.108), channel_id=1, replica_groups=mesh['dp'=32,'tensor'=4] {'dp','tensor'}, dimensions={1}, use_global_device_ids=true | all-gather | bytes 20640 | tf_op jit(solution)/shard_map/all_gather | solution.py:85
  188.2 1.0 slice_reduce_fusion
  189.2 1.1 fusion.25
  190.3 1.8 fusion.22
  195.1 90.5 %all_gather.30 = bf16[1024,256]{1,0:T(8,128)(2,1)S(1)} all-gather(bf16[32,256]{1,0:T(8,128)(2,1)S(1)} %convert_element_type.120), channel_id=1, replica_groups=mesh['dp'=32,'tensor'=4] {'dp'}, dimensions={0}, use_global_device_ids=true | all-gather | bytes 540672 | tf_op jit(solution)/shard_map/all_gather | solution.py:91
  285.7 2.7 convolution_bitcast_fusion.1
  288.5 1.1 multiply_convert_fusion.7
  289.6 1.8 fusion.55
  291.5 23.3 %reduce-scatter.8.cloned.1.call-done = f32[128,1024]{1,0:T(8,128)} async-done(((f32[512,1024]{1,0:T(8,128)}), f32[128,1024]{1,0:T(8,128)}) %reduce-scatter.8.cloned.1.call-update) | async-done | bytes 524304 | tf_op jit(solution)/shard_map/reduce_scatter | solution.py:111
  314.8 1.2 multiply_reduce_fusion.3
  316.6 1.5 multiply_convert_fusion.6
  318.1 1.6 convert_element_type.122
  321.1 1.7 broadcast_multiply_fusion
  323.7 16.2 %all-gather.12.cloned.1.call-done = bf16[512,1024]{1,0:T(8,128)(2,1)} async-done(((bf16[128,1024]{1,0:T(8,128)(2,1)}), bf16[512,1024]{1,0:T(8,128)(2,1)}) %all-gather.12.cloned.1.call-update) | async-done | bytes 1048592 | tf_op jit(solution)/shard_map/all_gather | solution.py:119
  339.9 88.3 %all-gather.14.cloned.1.call-done = bf16[2,1024,1152]{2,1,0:T(8,128)(2,1)} async-done(((bf16[2,32,1152]{2,1,0:T(8,128)(2,1)}), bf16[2,1024,1152]{2,1,0:T(8,128)(2,1)}) %all-gather.14.cloned.1.call-update) | async-done | bytes 4718608 | tf_op jit(solution)/shard_map/all_gather | solution.py:92
  428.2 7.4 convolution_bitcast_fusion
  435.6 13.2 all-gather.18.cloned.1.call-done
  448.8 76.9 %all-gather.16.cloned.1.call-done = bf16[1024,1152]{1,0:T(8,128)(2,1)} async-done(((bf16[32,1152]{1,0:T(8,128)(2,1)}), bf16[1024,1152]{1,0:T(8,128)(2,1)}) %all-gather.16.cloned.1.call-update) | async-done | bytes 2359312 | tf_op jit(solution)/shard_map/all_gather | solution.py:93
  525.8 6.7 fusion.4
  532.5 1.1 copy-done.51
  533.9 3.7 bitcast_convert_fusion.1
  537.6 17.0 %reduce-scatter.12.cloned.1.call-done = bf16[128,1024]{1,0:T(8,128)(2,1)} async-done(((bf16[512,1024]{1,0:T(8,128)(2,1)}), bf16[128,1024]{1,0:T(8,128)(2,1)}) %reduce-scatter.12.cloned.1.call-update) | async-done | bytes 262160 | tf_op jit(solution)/shard_map/reduce_scatter | solution.py:149
  554.7 1.8 fusion.21
  557.0 1.9 fusion.44
  559.2 21.7 %all-gather.20.cloned.1.call-done = bf16[512,1024]{1,0:T(8,128)(2,1)} async-done(((bf16[128,1024]{1,0:T(8,128)(2,1)}), bf16[512,1024]{1,0:T(8,128)(2,1)}) %all-gather.20.cloned.1.call-update) | async-done | bytes 1048592 | tf_op jit(solution)/shard_map/all_gather | solution.py:159
  580.9 2.6 convolution_convert_fusion.4
  583.5 4.6 convolution_convert_fusion.1
  589.7 2.6 multiply_reduce_fusion.2
  593.0 1.0 copy-done.47
  594.0 2.0 bitcast_convert_fusion
  596.1 4.6 convolution_convert_fusion.3
  600.8 6.0 fusion
  606.8 12.6 copy.113
  619.4 2.3 fusion.2
  621.7 2.6 copy.110
  626.2 142.7 %reduce-scatter.16.cloned.1.call-done = bf16[32,256]{1,0:T(8,128)(2,1)} async-done(((bf16[1024,256]{1,0:T(8,128)(2,1)}), bf16[32,256]{1,0:T(8,128)(2,1)}) %reduce-scatter.16.cloned.1.call-update) | async-done | bytes 16400 | tf_op jit(solution)/shard_map/reduce_scatter | solution.py:198
  768.9 1.4 multiply_subtract_fusion.3
  770.3 224.7 %reduce-scatter.18.cloned.1.call-done = bf16[32,1152]{1,0:T(8,128)(2,1)} async-done(((bf16[1024,1152]{1,0:T(8,128)(2,1)}), bf16[32,1152]{1,0:T(8,128)(2,1)}) %reduce-scatter.18.cloned.1.call-update) | async-done | bytes 73744 | tf_op jit(solution)/shard_map/reduce_scatter | solution.py:204
  995.0 1.7 multiply_subtract_fusion.1
  996.7 17.9 %reduce-scatter.14.cloned.1.call-done = bf16[128,1024]{1,0:T(8,128)(2,1)} async-done(((bf16[512,1024]{1,0:T(8,128)(2,1)}), bf16[128,1024]{1,0:T(8,128)(2,1)}) %reduce-scatter.14.cloned.1.call-update) | async-done | bytes 262160 | tf_op jit(solution)/shard_map/reduce_scatter | solution.py:179
  1014.6 1.2 fusion.24
  1015.8 68.4 %all-reduce.4 = f32[5,1024]{1,0:T(8,128)S(1)} all-reduce(f32[5,1024]{1,0:T(8,128)S(1)} %pad_maximum_fusion.6), channel_id=6, replica_groups=mesh['dp'=32,'tensor'=4] {'dp','tensor'}, use_global_device_ids=true, to_apply=%region_16.17.clone | all-reduce | flops 5120 | bytes 40960
  1085.0 2.2 fusion.17
  1087.2 334.6 %all-reduce.10.cloned.1.call-done = (bf16[3,1024,256]{2,0,1:T(4,128)(2,1)}, bf16[2,1024,1152]{2,0,1:T(2,128)(2,1)}) async-done(((bf16[3,1024,256]{2,0,1:T(4,128)(2,1)}, bf16[2,1024,1152]{2,0,1:T(2,128)(2,1)}), (bf16[3,1024,256]{2,0,1:T(4,128)(2,1)}, bf16[2,1024,1152]{2,0,1:T(2,128)(2,1)})) %all-reduce.10.cloned.1.call-update) | async-done | bytes 6291472
  1421.8 0.9 constant_dynamic-slice_fusion.1
  1422.7 1.0 constant_dynamic-slice_fusion
  1424.5 1.1 multiply_subtract_fusion
  (165 shorter events, 12.0 us)
Async XLA Ops:
  7.2 185.0 %copy-start.6 = (f32[3,32,256]{2,1,0:T(8,128)S(1)}, f32[3,32,256]{2,1,0:T(8,128)}, u32[]{:S(2)}) copy-start(f32[3,32,256]{2,1,0:T(8,128)} %param.22) | copy-start | bytes 294916
  7.2 185.9 %copy-start.49 = (s32[1,4]{1,0:T(1,128)S(1)}, s32[1,4]{1,0:T(1,128)}, u32[]{:S(2)}) copy-start(s32[1,4]{1,0:T(1,128)} %param.20) | copy-start | bytes 52
  7.2 186.7 %copy-start.14 = (f32[32,256]{1,0:T(8,128)S(1)}, f32[32,256]{1,0:T(8,128)}, u32[]{:S(2)}) copy-start(f32[32,256]{1,0:T(8,128)} %param.23) | copy-start | bytes 98308
  7.2 278.5 %all-gather.8.cloned.1.call-start = ((), (), s32[]{:S(2)}) async-start(), calls=%async_computation.6 | async-start | bytes 1310720 | tf_op jit(solution)/shard_map/all_gather | solution.py:98
  189.2 99.2 %copy-start.19 = (f32[1024]{0:T(1024)}, f32[1024]{0:T(1024)S(1)}, u32[]{:S(2)}) copy-start(f32[1024]{0:T(1024)S(1)} %get-tuple-element.93) | copy-start | bytes 12292
  192.1 93.6 %all-gather.10.cloned.1.call-start = ((), (), s32[]{:S(2)}) async-start(), calls=%async_computation.7 | async-start | bytes 1622016 | tf_op jit(solution)/shard_map/all_gather | solution.py:90
  192.9 122.0 %reduce-scatter.8.cloned.1.call-start = ((), (), s32[]{:S(2)}) async-start(), calls=%async_computation.8 | async-start | bytes 2621440 | tf_op jit(solution)/shard_map/reduce_scatter | solution.py:111
  194.2 94.2 %copy-start.27 = (f32[256]{0:T(256)}, f32[256]{0:T(256)S(1)}, u32[]{:S(2)}) copy-start(f32[256]{0:T(256)S(1)} %get-tuple-element.94) | copy-start | bytes 3076
  194.3 94.2 %copy-start.29 = (f32[256]{0:T(256)}, f32[256]{0:T(256)S(1)}, u32[]{:S(2)}) copy-start(f32[256]{0:T(256)S(1)} %get-tuple-element.95) | copy-start | bytes 3076
  194.3 94.2 %copy-start.31 = (f32[256]{0:T(256)}, f32[256]{0:T(256)S(1)}, u32[]{:S(2)}) copy-start(f32[256]{0:T(256)S(1)} %get-tuple-element.96) | copy-start | bytes 3076
  195.1 93.4 %copy-start.23 = (f32[512]{0:T(512)}, f32[512]{0:T(512)S(1)}, u32[]{:S(2)}) copy-start(f32[512]{0:T(512)S(1)} %get-tuple-element.127) | copy-start | bytes 6148
  195.1 93.4 %copy-start.24 = (f32[512]{0:T(512)}, f32[512]{0:T(512)S(1)}, u32[]{:S(2)}) copy-start(f32[512]{0:T(512)S(1)} %get-tuple-element.128) | copy-start | bytes 6148
  289.6 25.2 %copy-start = (bf16[128,1024]{1,0:T(8,128)(2,1)S(1)}, bf16[128,1024]{1,0:T(8,128)(2,1)}, u32[]{:S(2)}) copy-start(bf16[128,1024]{1,0:T(8,128)(2,1)} %param.18) | copy-start | bytes 786436
  291.4 31.5 %copy-start.5 = (f32[32,1152]{1,0:T(8,128)S(1)}, f32[32,1152]{1,0:T(8,128)}, u32[]{:S(2)}) copy-start(f32[32,1152]{1,0:T(8,128)} %param.25) | copy-start | bytes 442372
  291.5 48.4 %all-gather.12.cloned.1.call-start = ((), (), s32[]{:S(2)}) async-start(), calls=%async_computation.9 | async-start | bytes 1310720 | tf_op jit(solution)/shard_map/all_gather | solution.py:119
  318.1 110.1 %all-gather.14.cloned.1.call-start = ((), (), s32[]{:S(2)}) async-start(), calls=%async_computation.10 | async-start | bytes 4866048 | tf_op jit(solution)/shard_map/all_gather | solution.py:92
  319.8 129.0 %all-gather.18.cloned.1.call-start = ((), (), s32[]{:S(2)}) async-start(), calls=%async_computation.13 | async-start | bytes 1310720 | tf_op jit(solution)/shard_map/all_gather | solution.py:141
  322.9 202.9 %all-gather.16.cloned.1.call-start = ((), (), s32[]{:S(2)}) async-start(), calls=%async_computation.11 | async-start | bytes 2433024 | tf_op jit(solution)/shard_map/all_gather | solution.py:93
  323.6 231.1 %reduce-scatter.12.cloned.1.call-start = ((), (), s32[]{:S(2)}) async-start(), calls=%async_computation.14 | async-start | bytes 1310720 | tf_op jit(solution)/shard_map/reduce_scatter | solution.py:149
  537.6 43.3 %all-gather.20.cloned.1.call-start = ((), (), s32[]{:S(2)}) async-start(), calls=%async_computation.15 | async-start | bytes 1310720 | tf_op jit(solution)/shard_map/all_gather | solution.py:159
  559.0 209.9 %reduce-scatter.16.cloned.1.call-start = ((), (), s32[]{:S(2)}) async-start(), calls=%async_computation.17 | async-start | bytes 540672 | tf_op jit(solution)/shard_map/reduce_scatter | solution.py:198
  583.5 411.5 %reduce-scatter.18.cloned.1.call-start = ((), (), s32[]{:S(2)}) async-start(), calls=%async_computation.18 | async-start | bytes 2433024 | tf_op jit(solution)/shard_map/reduce_scatter | solution.py:204
  588.2 426.4 %reduce-scatter.14.cloned.1.call-start = ((), (), s32[]{:S(2)}) async-start(), calls=%async_computation.16 | async-start | bytes 1310720 | tf_op jit(solution)/shard_map/reduce_scatter | solution.py:179
  596.1 488.9 %reduce-scatter.10.cloned.1.call-start = ((), (), s32[]{:S(2)}) async-start(), calls=%async_computation.12 | async-start | bytes 1310720 | tf_op jit(solution)/shard_map/reduce_scatter | solution.py:131
  600.8 821.1 %all-reduce.10.cloned.1.call-start = ((), (), s32[]{:S(2)}) async-start(), calls=%async_computation.19 | async-start | bytes 13631488
  624.3 144.7 %copy-start.15 = (f32[32,256]{1,0:T(8,128)S(1)}, f32[32,256]{1,0:T(8,128)}, u32[]{:S(2)}) copy-start(f32[32,256]{1,0:T(8,128)} %param.23) | copy-start | bytes 98308
  624.3 144.7 %copy-start.21 = (f32[32,256]{1,0:T(8,128)S(1)}, f32[32,256]{1,0:T(8,128)}, u32[]{:S(2)}) copy-start(f32[32,256]{1,0:T(8,128)} %param.31) | copy-start | bytes 98308
  624.3 144.7 %copy-start.22 = (f32[32,256]{1,0:T(8,128)S(1)}, f32[32,256]{1,0:T(8,128)}, u32[]{:S(2)}) copy-start(f32[32,256]{1,0:T(8,128)} %param.30) | copy-start | bytes 98308
  624.3 370.7 %copy-start.12 = (f32[32,1152]{1,0:T(8,128)S(1)}, f32[32,1152]{1,0:T(8,128)}, u32[]{:S(2)}) copy-start(f32[32,1152]{1,0:T(8,128)} %param.35) | copy-start | bytes 442372
  624.3 370.7 %copy-start.13 = (f32[32,1152]{1,0:T(8,128)S(1)}, f32[32,1152]{1,0:T(8,128)}, u32[]{:S(2)}) copy-start(f32[32,1152]{1,0:T(8,128)} %param.34) | copy-start | bytes 442372
  624.3 390.2 %copy-start.20 = (f32[1024]{0:T(1024)S(1)}, f32[1024]{0:T(1024)}, u32[]{:S(2)}) copy-start(f32[1024]{0:T(1024)} %copy-done.19) | copy-start | bytes 12292
  624.3 390.2 %copy-start.38 = (f32[128]{0:T(128)S(1)}, f32[128]{0:T(128)}, u32[]{:S(2)}) copy-start(f32[128]{0:T(128)} %copy-done.37) | copy-start | bytes 1540
  624.3 391.5 %copy-start.25 = (f32[1024]{0:T(1024)S(1)}, f32[1024]{0:T(1024)}, u32[]{:S(2)}) copy-start(f32[1024]{0:T(1024)} %get-tuple-element.85) | copy-start | bytes 12292
  624.4 459.9 %copy-start.26 = (f32[5,8]{1,0:T(8,128)S(1)}, f32[5,8]{1,0:T(8,128)}, u32[]{:S(2)}) copy-start(f32[5,8]{1,0:T(8,128)} %param.21) | copy-start | bytes 484
  624.4 459.8 %copy-start.42 = (f32[5,8]{1,0:T(8,128)S(1)}, f32[5,8]{1,0:T(8,128)}, u32[]{:S(2)}) copy-start(f32[5,8]{1,0:T(8,128)} %param.27) | copy-start | bytes 484
  624.4 459.8 %copy-start.43 = (f32[5,8]{1,0:T(8,128)S(1)}, f32[5,8]{1,0:T(8,128)}, u32[]{:S(2)}) copy-start(f32[5,8]{1,0:T(8,128)} %param.26) | copy-start | bytes 484
  624.4 460.5 %copy-start.1 = (bf16[128,1024]{1,0:T(8,128)(2,1)S(1)}, bf16[128,1024]{1,0:T(8,128)(2,1)}, u32[]{:S(2)}) copy-start(bf16[128,1024]{1,0:T(8,128)(2,1)} %param.19) | copy-start | bytes 786436
  624.4 460.5 %copy-start.2 = (bf16[128,1024]{1,0:T(8,128)(2,1)S(1)}, bf16[128,1024]{1,0:T(8,128)(2,1)}, u32[]{:S(2)}) copy-start(bf16[128,1024]{1,0:T(8,128)(2,1)} %reduce-scatter.12.cloned.1.call-done) | copy-start | bytes 786436
  624.4 460.5 %copy-start.16 = (f32[1024]{0:T(1024)S(1)}, f32[1024]{0:T(1024)}, u32[]{:S(2)}) copy-start(f32[1024]{0:T(1024)} %get-tuple-element.92) | copy-start | bytes 12292
  624.4 460.5 %copy-start.34 = (f32[128]{0:T(128)S(1)}, f32[128]{0:T(128)}, u32[]{:S(2)}) copy-start(f32[128]{0:T(128)} %copy-done.33) | copy-start | bytes 1540
  624.4 460.5 %copy-start.36 = (bf16[128]{0:T(256)(128)(2,1)S(1)}, bf16[128]{0:T(256)(128)(2,1)}, u32[]{:S(2)}) copy-start(bf16[128]{0:T(256)(128)(2,1)} %copy-done.35) | copy-start | bytes 772
  624.4 460.5 %copy-start.45 = (f32[128]{0:T(128)S(1)}, f32[128]{0:T(128)}, u32[]{:S(2)}) copy-start(f32[128]{0:T(128)} %copy-done.44) | copy-start | bytes 1540
  770.3 653.4 %copy-start.7 = (f32[3,32,256]{2,1,0:T(8,128)S(1)}, f32[3,32,256]{2,1,0:T(8,128)}, u32[]{:S(2)}) copy-start(f32[3,32,256]{2,1,0:T(8,128)} %param.22) | copy-start | bytes 294916
  770.3 653.4 %copy-start.17 = (f32[3,32,256]{2,1,0:T(8,128)S(1)}, f32[3,32,256]{2,1,0:T(8,128)}, u32[]{:S(2)}) copy-start(f32[3,32,256]{2,1,0:T(8,128)} %param.29) | copy-start | bytes 294916
  770.3 653.4 %copy-start.18 = (f32[3,32,256]{2,1,0:T(8,128)S(1)}, f32[3,32,256]{2,1,0:T(8,128)}, u32[]{:S(2)}) copy-start(f32[3,32,256]{2,1,0:T(8,128)} %param.28) | copy-start | bytes 294916
  996.7 427.8 %copy-start.3 = (f32[2,32,1152]{2,1,0:T(8,128)S(1)}, f32[2,32,1152]{2,1,0:T(8,128)}, u32[]{:S(2)}) copy-start(f32[2,32,1152]{2,1,0:T(8,128)} %param.24) | copy-start | bytes 884740
  996.7 427.8 %copy-start.8 = (f32[2,32,1152]{2,1,0:T(8,128)S(1)}, f32[2,32,1152]{2,1,0:T(8,128)}, u32[]{:S(2)}) copy-start(f32[2,32,1152]{2,1,0:T(8,128)} %param.33) | copy-start | bytes 884740
  996.7 427.8 %copy-start.9 = (f32[2,32,1152]{2,1,0:T(8,128)S(1)}, f32[2,32,1152]{2,1,0:T(8,128)}, u32[]{:S(2)}) copy-start(f32[2,32,1152]{2,1,0:T(8,128)} %param.32) | copy-start | bytes 884740
  (19 other events, 52.2 us)
Sparse Core Ops, SparseCore 0:
  192.2 14.4 all-gather.7
  210.3 70.3 all-gather.9
  291.6 23.2 reduce-scatter.7
  318.2 21.6 all-gather.11
  343.8 84.3 all-gather.13
  430.4 18.3 all-gather.17
  452.9 72.8 all-gather.15
  537.7 16.9 reduce-scatter.11
  559.1 21.7 all-gather.19
  583.6 185.2 reduce-scatter.15
  774.7 220.1 reduce-scatter.17
  997.4 17.1 reduce-scatter.13
  1017.0 21.0 reduce-scatter.9
  1040.7 381.0 all-reduce.9
where the time goes:
time: 1430 us
  waiting for transfers between devices  977 us (68%)
  blocking collectives  339 us (24%)
  matrix products  46.9 us (3%)
  other arithmetic  27.1 us (2%)
  local copies, waits for them, and re-layouts  26.1 us (2%)
  between operations  15.2 us (1%)
    unnamed x15, waiting for transfers between devices  335 us
    reduce_scatter x1, waiting for transfers between devices, per_device(): lax.psum_scatter(down_grad.astype(jnp.bfloat16), 'dp', scatter_dimension=...  225 us
    all_gather x1, blocking collectives, per_device(): small_all = lax.all_gather(small, ('dp', 'tensor'), axis=1, tiled=True)  180 us
    reduce_scatter x1, waiting for transfers between devices, per_device(): lax.psum_scatter(out_grad.astype(jnp.bfloat16), 'dp', scatter_dimension=0...  143 us
    all_gather x1, blocking collectives, per_device(): lax.all_gather(mix_out.astype(jnp.bfloat16), 'dp', axis=0, tiled=True)  90.5 us
    all_gather x1, waiting for transfers between devices, per_device(): lax.all_gather(ffn_gate_up.astype(jnp.bfloat16), 'dp', axis=1, tiled=True)  88.3 us
    all_gather x1, waiting for transfers between devices, per_device(): lax.all_gather(ffn_down.astype(jnp.bfloat16), 'dp', axis=0, tiled=True)  76.9 us
    unnamed x1, blocking collectives  68.4 us
  transfers between devices with their start and end apart: 14, of which 11 were waited for; matrix products, arithmetic and copies ran while one was open for 4% of the time, Pallas kernels for 0%

commit v1 on v0

v1 whole, which is shorter than its diff:
```python
import functools

import jax
import jax.numpy as jnp
from jax import lax
from jax.experimental import pallas as pl
from jax.experimental.pallas import tpu as pltpu
from jax.sharding import PartitionSpec as P

STEP = 10
NORM_EPSILON = 1e-05
BETA_FIRST = 0.9
BETA_SECOND = 0.95
ADAM_EPSILON = 1e-08
DECAY_RATE = 0.1
RATE_PROJ = 0.1
RATE_DOWN = 0.045
RATE_SMALL = 0.6

MESH = pl.DeviceIdType.MESH
F32 = jnp.float32
BF16 = jnp.bfloat16

D = 1024
ROWS = 512
BLOCK = 128
CH = 256
HID = 1152
TILE = 128
TILES = HID // TILE
OUT_AT = 3 * CH
GU_AT = 4 * CH
DOWN_AT = GU_AT + 2 * HID
WIDE = DOWN_AT + HID
PARTS = ((0, GU_AT), (GU_AT, 2 * HID), (DOWN_AT, HID))
NZ, NY, NX, SHARD = 4, 2, 4, 32
HALF = SHARD // 2


def mm(a, b):
    return lax.dot_general(a, b, (((1,), (0,)), ((), ())), preferred_element_type=F32)


def mm_nt(a, b):
    return lax.dot_general(a, b, (((1,), (1,)), ((), ())), preferred_element_type=F32)


def loop(n, body):
    lax.fori_loop(0, n, lambda i, carry: (body(i), carry)[1], 0)


def at_lane(i, width):
    return pl.ds(pl.multiple_of(i * width, width), width)


class Links:
    def __init__(self, send, recv):
        self.send, self.recv, self.used, self.open = send, recv, 0, []

    def take(self, n=1):
        first = self.used
        self.used += n
        return first

    def copy(self, src, dst, to, slot):
        return pltpu.make_async_remote_copy(
            src_ref=src,
            dst_ref=dst,
            send_sem=self.send.at[slot],
            recv_sem=self.recv.at[slot],
            device_id=to,
            device_id_type=MESH,
        )

    def push(self, src, dst, to):
        c = self.copy(src, dst, to, self.take())
        c.start()
        self.open.append(c)
        return c


def arrived(copies):
    for c in copies:
        c.wait_recv()


def train_kernel(
    lens,
    tok_in,
    cot_in,
    small_in,
    win,
    wout,
    wgu,
    wdn,
    bo_out,
    tg_out,
    gs_out,
    sg_out,
    w,
    g,
    tok,
    cot,
    one,
    two,
    rmid,
    masks,
    pj,
    conv,
    gated,
    gp,
    gu,
    hid,
    gg,
    mid,
    gmid,
    sml,
    st,
    sr,
    sm,
    sgr,
    gr,
    gc,
    gacc,
    ps,
    pr,
    po,
    qs,
    qr,
    r2s1,
    r2s2z,
    r2s2x,
    r1s1,
    r1s2,
    ry,
    send_sem,
    recv_sem,
):
    dp = lax.axis_index("dp")
    t = lax.axis_index("tensor")
    z, yh, x = dp // 8, (dp // 4) % 2, dp % 4
    ty, tc = t // 2, t % 2
    zp, zm, zo = (z + 1) % 4, (z + 3) % 4, (z + 2) % 4
    xp, xm, xo = (x + 1) % 4, (x + 3) % 4, (x + 2) % 4

    def at(zz, yy, xx):
        return (zz * 8 + yy * 4 + xx, t)

    to_y = at(z, 1 - yh, x)
    to_xp, to_xm = at(z, yh, xp), at(z, yh, xm)
    to_zp, to_zm = at(zp, yh, x), at(zm, yh, x)
    x1 = x + 1 - 2 * (x % 2)
    z1 = z + 1 - 2 * (z % 2)
    to_x1, to_x3 = at(z, yh, x1), at(z, yh, 3 - x)
    to_z1, to_z3 = at(z1, yh, x), at(3 - z, yh, x)
    to_core = (dp, ty * 2 + 1 - tc)
    to_far = (dp, (1 - ty) * 2 + tc)
    links = Links(send_sem, recv_sem)

    for j in range(3):
        w[z, yh, x, :, j * CH : (j + 1) * CH] = win[j].astype(BF16)
    w[z, yh, x, :, OUT_AT : OUT_AT + CH] = wout[...].astype(BF16)
    for i in range(TILES):
        for j in range(2):
            lo = GU_AT + (2 * i + j) * TILE
            w[z, yh, x, :, lo : lo + TILE] = wgu[j, :, i * TILE : (i + 1) * TILE].astype(BF16)
    w[z, yh, x, :, DOWN_AT:WIDE] = wdn[...].astype(BF16)
    tok[ty, tc] = tok_in[...]
    st[0] = small_in[...]

    row = lax.broadcasted_iota(jnp.int32, (ROWS, TILE), 0)
    start = jnp.zeros((ROWS, TILE), jnp.int32)
    run = jnp.int32(0)
    for k in range(lens.shape[1]):
        run = run + lens[0, k]
        start = jnp.where(row >= run, run, start)
    dist = row - start
    masks[0] = jnp.where(dist >= 1, 1.0, 0.0)
    masks[1] = jnp.where(dist >= 2, 1.0, 0.0)
    my_row = lax.broadcasted_iota(jnp.int32, (BLOCK, D), 0) + t * BLOCK
    cot[ty, tc] = jnp.where(my_row < run, cot_in[...].astype(F32), 0.0).astype(BF16)

    barrier = pltpu.get_barrier_semaphore()
    peers = (to_y, to_xp, to_xm, to_zp, to_zm, to_core, to_far)
    for to in peers:
        pl.semaphore_signal(barrier, inc=1, device_id=to, device_id_type=MESH)
    pl.semaphore_wait(barrier, len(peers))

    lo_half, hi_half = pl.ds(0, HALF), pl.ds(HALF, HALF)

    def cols(part):
        return pl.ds(PARTS[part][0], PARTS[part][1])

    def same(ref, to):
        return links.push(ref, ref, to)

    def wy(p):
        return same(w.at[z, yh, x, :, cols(p)], to_y)

    def w1a(p):
        a, b = w.at[z, :, x, lo_half, cols(p)], w.at[z, :, x, hi_half, cols(p)]
        return [same(a, to_xp), same(a, to_xm), same(b, to_zp), same(b, to_zm)]

    def w1b(p):
        return [
            same(w.at[z, 0, xm, lo_half, cols(p)], to_xp),
            same(w.at[z, 1, xp, lo_half, cols(p)], to_xm),
            same(w.at[zm, 0, x, hi_half, cols(p)], to_zp),
            same(w.at[zp, 1, x, hi_half, cols(p)], to_zm),
        ]

    def w2a(p):
        a, b = w.at[z, :, :, lo_half, cols(p)], w.at[:, :, x, hi_half, cols(p)]
        return [same(a, to_zp), same(a, to_zm), same(b, to_xp), same(b, to_xm)]

    def w2b(p):
        return [
            same(w.at[zm, 0, :, lo_half, cols(p)], to_zp),
            same(w.at[zp, 1, :, lo_half, cols(p)], to_zm),
            same(w.at[:, 0, xm, hi_half, cols(p)], to_xp),
            same(w.at[:, 1, xp, hi_half, cols(p)], to_xm),
        ]

    def rows_start(ref):
        mine = ref.at[ty, tc]
        return [same(mine, to_far), same(mine, to_core)]

    def rows_relay(ref, copies):
        copies[0].wait_recv()
        copies.append(same(ref.at[1 - ty, tc], to_core))

    def rows_wait(copies):
        arrived(copies[1:])

    def sum_start(u, lhs, lo, k):
        first = links.take(NZ)

        def step(i):
            wt = w[i, :, :, :, lo : lo + k].reshape(D // NZ, k)
            a = lhs[:, 1 - tc].reshape(2 * BLOCK, k)
            ps[u, i] = mm_nt(a, wt).astype(BF16).reshape(2, BLOCK, CH)
            links.copy(ps.at[u, i], pr.at[u, i], to_core, first + i).start()
            b = lhs[:, tc].reshape(2 * BLOCK, k)
            po[u, i] = mm_nt(b, wt).reshape(2, BLOCK, CH)

        loop(NZ, step)
        links.open += [links.copy(ps.at[u, i], pr.at[u, i], to_core, first + i) for i in range(NZ)]
        return first

    def sum_cross(u, first):
        second = links.take(NZ)

        def step(i):
            links.copy(ps.at[u, i], pr.at[u, i], to_core, first + i).wait_recv()
            other = po[u, i, 1 - ty] + pr[u, i, 1 - ty].astype(F32)
            qs[u, i] = other.astype(BF16)
            links.copy(qs.at[u, i], qr.at[u, i], to_far, second + i).start()
            po[u, i, ty] = po[u, i, ty] + pr[u, i, ty].astype(F32)

        loop(NZ, step)
        links.open += [links.copy(qs.at[u, i], qr.at[u, i], to_far, second + i) for i in range(NZ)]
        return second

    def sum_wait(u, second):
        for i in range(NZ):
            links.copy(qs.at[u, i], qr.at[u, i], to_far, second + i).wait_recv()

    def sum_rows(u, lo, n):
        return jnp.concatenate(
            [po[u, i, ty, pl.ds(lo, n), :] + qr[u, i, pl.ds(lo, n), :].astype(F32) for i in range(NZ)],
            axis=1,
        )

    def add_to(dst, src):
        dst[...] = (dst[...].astype(F32) + src[...].astype(F32)).astype(BF16)

    def g2a(p):
        c = cols(p)
        return [
            links.push(g.at[zo, 0, :, lo_half, c], r2s1.at[0, 0, :, :, c], to_zm),
            links.push(g.at[zo, 1, :, lo_half, c], r2s1.at[0, 1, :, :, c], to_zp),
            links.push(g.at[:, 0, xo, hi_half, c], r2s1.at[1, 0, :, :, c], to_xm),
            links.push(g.at[:, 1, xo, hi_half, c], r2s1.at[1, 1, :, :, c], to_xp),
        ]

    def g2b(p, copies):
        c = cols(p)
        out = []
        for k, (y, zz, to) in enumerate(((0, zm, to_zm), (1, zp, to_zp))):
            copies[k].wait_recv()
            loop(4, lambda i: add_to(g.at[zz, y, i, lo_half, c], r2s1.at[0, y, i, :, c]))
            out.append(links.push(g.at[zz, :, :, lo_half, c], r2s2z.at[y, :, :, :, c], to))
        for k, (y, xx, to) in enumerate(((0, xm, to_xm), (1, xp, to_xp))):
            copies[2 + k].wait_recv()
            loop(4, lambda i: add_to(g.at[i, y, xx, hi_half, c], r2s1.at[1, y, i, :, c]))
            out.append(links.push(g.at[:, :, xx, hi_half, c], r2s2x.at[y, :, :, :, c], to))
        return out

    def add_two(dst, a, b):
        total = dst[...].astype(F32) + a[...].astype(F32) + b[...].astype(F32)
        dst[...] = total.astype(BF16)

    def g1a(p, copies):
        c = cols(p)
        arrived(copies[:2])
        loop(
            8,
            lambda i: add_two(
                g.at[z, i // 4, i % 4, lo_half, c],
                r2s2z.at[0, i // 4, i % 4, :, c],
                r2s2z.at[1, i // 4, i % 4, :, c],
            ),
        )
        out = [
            links.push(g.at[z, 0, xo, lo_half, c], r1s1.at[0, 0, :, c], to_xm),
            links.push(g.at[z, 1, xo, lo_half, c], r1s1.at[0, 1, :, c], to_xp),
        ]
        arrived(copies[2:])
        loop(
            8,
            lambda i: add_two(
                g.at[i // 2, i % 2, x, hi_half, c],
                r2s2x.at[0, i // 2, i % 2, :, c],
                r2s2x.at[1, i // 2, i % 2, :, c],
            ),
        )
        return out + [
            links.push(g.at[zo, 0, x, hi_half, c], r1s1.at[1, 0, :, c], to_zm),
            links.push(g.at[zo, 1, x, hi_half, c], r1s1.at[1, 1, :, c], to_zp),
        ]

    def g1b(p, copies):
        c = cols(p)
        out = []
        for k, (y, xx, to) in enumerate(((0, xm, to_xm), (1, xp, to_xp))):
            copies[k].wait_recv()
            add_to(g.at[z, y, xx, lo_half, c], r1s1.at[0, y, :, c])
            out.append(links.push(g.at[z, :, xx, lo_half, c], r1s2.at[0, y, :, :, c], to))
        for k, (y, zz, to) in enumerate(((0, zm, to_zm), (1, zp, to_zp))):
            copies[2 + k].wait_recv()
            add_to(g.at[zz, y, x, hi_half, c], r1s1.at[1, y, :, c])
            out.append(links.push(g.at[zz, :, x, hi_half, c], r1s2.at[1, y, :, :, c], to))
        return out

    def gy(p, copies):
        c = cols(p)
        arrived(copies)
        for h, rows in enumerate((lo_half, hi_half)):
            loop(
                2,
                lambda y: add_two(
                    g.at[z, y, x, rows, c], r1s2.at[h, 0, y, :, c], r1s2.at[h, 1, y, :, c]
                ),
            )
        return links.push(g.at[z, 1 - yh, x, :, c], ry.at[:, c], to_y)

    def gend(p, copy):
        c = cols(p)
        copy.wait_recv()
        gs_out[:, c] = g[z, yh, x, :, c].astype(F32) + ry[:, c].astype(F32)

    s_far = links.push(st.at[0], sr.at[0], to_far)
    y0 = wy(0)
    tok_c = rows_start(tok)
    y1 = wy(1)
    y2 = wy(2)
    s_far.wait_recv()
    st[1] = st[0] + sr[0]
    s_core = links.push(st.at[1], sr.at[1], to_core)
    y0.wait_recv()
    a1a = w1a(0)
    s_core.wait_recv()
    st[2] = st[1] + sr[1]
    s_x1 = links.push(st.at[2], sr.at[2], to_x1)
    rows_relay(tok, tok_c)
    arrived(a1a)
    a1b = w1b(0)
    s_x1.wait_recv()
    st[3] = st[2] + sr[2]
    s_x3 = links.push(st.at[3], sr.at[3], to_x3)
    y1.wait_recv()
    b1a = w1a(1)
    s_x3.wait_recv()
    sm[z, yh] = st[3] + sr[3]
    s_y = same(sm.at[z, yh], to_y)
    arrived(a1b)
    a2a = w2a(0)
    y2.wait_recv()
    c1a = w1a(2)
    s_y.wait_recv()
    s_z1 = same(sm.at[z], to_z1)
    cot_c = rows_start(cot)
    s_z1.wait_recv()
    s_z3 = same(sm.at[pl.ds((z // 2) * 2, 2)], to_z3)
    arrived(b1a)
    b1b = w1b(1)
    s_z3.wait_recv()
    for k in range(8):
        sml[:, k * TILE : (k + 1) * TILE] = sm[k // 2, k % 2]
    rows_wait(tok_c)

    def norm_in(i):
        a, b, r = i // 8, (i // 4) % 2, (i % 4) * 32
        v = tok[a, b, pl.ds(r, 32), :].astype(F32)
        inv = lax.rsqrt(jnp.mean(v * v, axis=1, keepdims=True) + NORM_EPSILON)
        one[a, b, pl.ds(r, 32), :] = (v * inv * sml[0:1, :]).astype(BF16)

    loop(16, norm_in)
    arrived(a2a)
    a2b = w2b(0)
    arrived(b1b)
    b2a = w2a(1)
    arrived(c1a)
    c1b = w1b(2)
    rows_relay(cot, cot_c)
    arrived(a2b)

    def proj(j):
        pj[j] = mm(one[...].reshape(ROWS, D), w[:, :, :, :, at_lane(j, CH)].reshape(D, CH))

    loop(3, proj)
    arrived(c1b)
    c2a = w2a(2)

    def taps(k, lanes):
        return sml[2 + k : 3 + k, lanes]

    for q in range(2):
        lanes = slice(q * TILE, (q + 1) * TILE)
        own = at_lane(t * 2 + q, TILE)
        mixed = pj[0, :, lanes] * pj[2, :, lanes]
        before_one = pltpu.roll(mixed, 1, 0) * masks[0]
        before_two = pltpu.roll(mixed, 2, 0) * masks[1]
        v = taps(0, own) * mixed + taps(1, own) * before_one + taps(2, own) * before_two
        conv[:, lanes] = v
        gated[:, :, :, lanes] = (pj[1, :, lanes] * v).astype(BF16).reshape(2, 2, BLOCK, TILE)

    m_first = sum_start(0, gated, OUT_AT, CH)
    m_second = sum_cross(0, m_first)
    sum_wait(0, m_second)

    def norm_mid(i):
        r = i * 32
        v = tok[ty, tc, pl.ds(r, 32), :].astype(F32) + sum_rows(0, r, 32)
        mid[pl.ds(r, 32), :] = v
        inv = lax.rsqrt(jnp.mean(v * v, axis=1, keepdims=True) + NORM_EPSILON)
        two[ty, tc, pl.ds(r, 32), :] = (v * inv * sml[1:2, :]).astype(BF16)

    loop(4, norm_mid)
    two_c = rows_start(two)
    arrived(b2a)
    b2b = w2b(1)
    rows_relay(two, two_c)
    rows_wait(two_c)
    rows_wait(cot_c)
    arrived(b2b)

    def gate_up(i):
        lanes = pl.ds(pl.multiple_of(GU_AT + i * CH, CH), CH)
        v = mm(two[...].reshape(ROWS, D), w[:, :, :, :, lanes].reshape(D, CH))
        gate, up = v[:, :TILE], v[:, TILE:]
        s = jax.nn.sigmoid(gate)
        act = gate * s
        hid[:, :, :, at_lane(i, TILE)] = (act * up).astype(BF16).reshape(2, 2, BLOCK, TILE)
        gu[i, :, :TILE] = up * s * (1.0 + gate * (1.0 - s))
        gu[i, :, TILE:] = act

    loop(TILES, gate_up)
    arrived(c2a)
    c2b = w2b(2)

    def wide(v):
        return v.reshape(NY, NX, SHARD, v.shape[1])

    def down_grad(i):
        a = cot[:, :, :, at_lane(i, CH)].reshape(ROWS, CH).T
        g[i, :, :, :, DOWN_AT:WIDE] = wide(mm(a, hid[...].reshape(ROWS, HID)).astype(BF16))

    loop(NZ, down_grad)
    gc2a = g2a(2)
    arrived(c2b)

    def back_tile(k, gh):
        v = gu[k]
        gg[:, :, :, at_lane(2 * k, TILE)] = (gh * v[:, :TILE]).astype(BF16).reshape(2, 2, BLOCK, TILE)
        gg[:, :, :, at_lane(2 * k + 1, TILE)] = (
            (gh * v[:, TILE:]).astype(BF16).reshape(2, 2, BLOCK, TILE)
        )

    def grad_hidden(i):
        lanes = pl.ds(pl.multiple_of(DOWN_AT + i * CH, TILE), CH)
        v = mm(cot[...].reshape(ROWS, D), w[:, :, :, :, lanes].reshape(D, CH))
        back_tile(2 * i, v[:, :TILE])
        back_tile(2 * i + 1, v[:, TILE:])

    loop(TILES // 2, grad_hidden)
    back_tile(
        TILES - 1,
        mm(cot[...].reshape(ROWS, D), w[:, :, :, :, WIDE - TILE : WIDE].reshape(D, TILE)),
    )
    n_first = sum_start(1, gg, GU_AT, 2 * HID)
    n_second = sum_cross(1, n_first)

    def gate_up_grad(i):
        a = two[:, :, :, at_lane(i, CH)].reshape(ROWS, CH).T
        for q in range(3):
            lo = q * 3 * CH
            b = gg[:, :, :, lo : lo + 3 * CH].reshape(ROWS, 3 * CH)
            g[i, :, :, :, GU_AT + lo : GU_AT + lo + 3 * CH] = wide(mm(a, b).astype(BF16))

    loop(NZ, gate_up_grad)
    gb2a = g2a(1)
    sum_wait(1, n_second)
    gacc[...] = jnp.zeros_like(gacc)

    def norm_two_back(i):
        r = i * 32
        gn = sum_rows(1, r, 32)
        v = mid[pl.ds(r, 32), :]
        inv = lax.rsqrt(jnp.mean(v * v, axis=1, keepdims=True) + NORM_EPSILON)
        unit = v * inv
        gacc[1:2, :] += jnp.sum(gn * unit, axis=0, keepdims=True)
        scaled = gn * sml[1:2, :]
        inner = jnp.mean(scaled * unit, axis=1, keepdims=True)
        out = cot[ty, tc, pl.ds(r, 32), :].astype(F32) + inv * (scaled - unit * inner)
        gmid[pl.ds(r, 32), :] = out
        rmid[ty, tc, pl.ds(r, 32), :] = out.astype(BF16)

    loop(4, norm_two_back)
    mid_c = rows_start(rmid)
    gc2b = g2b(2, gc2a)
    rows_relay(rmid, mid_c)
    o_first = sum_start(2, hid, DOWN_AT, HID)
    rows_wait(mid_c)
    gc1a = g1a(2, gc2b)
    gb2b = g2b(1, gb2a)

    pj_c = mm(rmid[...].reshape(ROWS, D), w[:, :, :, :, OUT_AT : OUT_AT + CH].reshape(D, CH))
    pg = pj_c
    for q in range(2):
        lanes = slice(q * TILE, (q + 1) * TILE)
        own = at_lane(t * 2 + q, TILE)
        gate_b, gate_c, values = pj[0, :, lanes], pj[1, :, lanes], pj[2, :, lanes]
        mixed = gate_b * values
        gv = pg[:, lanes]
        grad_c = gv * conv[:, lanes]
        grad_conv = gv * gate_c
        one_grad, two_grad = grad_conv * masks[0], grad_conv * masks[1]
        gacc[2:3, own] = jnp.sum(grad_conv * mixed, axis=0, keepdims=True)
        gacc[3:4, own] = jnp.sum(one_grad * pltpu.roll(mixed, 1, 0), axis=0, keepdims=True)
        gacc[4:5, own] = jnp.sum(two_grad * pltpu.roll(mixed, 2, 0), axis=0, keepdims=True)
        grad_mixed = (
            taps(0, own) * grad_conv
            + taps(1, own) * pltpu.roll(one_grad, ROWS - 1, 0)
            + taps(2, own) * pltpu.roll(two_grad, ROWS - 2, 0)
        )
        for j, v in enumerate((grad_mixed * values, grad_c, grad_mixed * gate_b)):
            lo = j * CH + q * TILE
            gp[:, :, :, lo : lo + TILE] = v.astype(BF16).reshape(2, 2, BLOCK, TILE)

    i_first = sum_start(3, gp, 0, 3 * CH)

    def mix_grad(i):
        a = one[:, :, :, at_lane(i, CH)].reshape(ROWS, CH).T
        g[i, :, :, :, :OUT_AT] = wide(mm(a, gp[...].reshape(ROWS, 3 * CH)).astype(BF16))
        b = rmid[:, :, :, at_lane(i, CH)].reshape(ROWS, CH).T
        g[i, :, :, :, OUT_AT:GU_AT] = wide(mm(b, gated[...].reshape(ROWS, CH)).astype(BF16))

    loop(NZ, mix_grad)
    ga2a = g2a(0)
    i_second = sum_cross(3, i_first)
    gc1b = g1b(2, gc1a)
    o_second = sum_cross(2, o_first)
    sum_wait(3, i_second)

    def norm_one_back(i):
        r = i * 32
        gn = sum_rows(3, r, 32)
        v = tok[ty, tc, pl.ds(r, 32), :].astype(F32)
        inv = lax.rsqrt(jnp.mean(v * v, axis=1, keepdims=True) + NORM_EPSILON)
        unit = v * inv
        gacc[0:1, :] += jnp.sum(gn * unit, axis=0, keepdims=True)
        scaled = gn * sml[0:1, :]
        inner = jnp.mean(scaled * unit, axis=1, keepdims=True)
        tg_out[pl.ds(r, 32), :] = gmid[pl.ds(r, 32), :] + inv * (scaled - unit * inner)

    loop(4, norm_one_back)
    for k in range(8):
        sgr[k // 2, k % 2] = gacc[:, k * TILE : (k + 1) * TILE]
    pair = (z // 2) * 2
    u_z3 = links.push(sgr.at[pl.ds(2 - pair, 2)], gr.at[pl.ds(0, 2)], to_z3)
    ga2b = g2b(0, ga2a)
    u_z3.wait_recv()
    sgr[pl.ds(pair, 2)] = sgr[pl.ds(pair, 2)] + gr[0:2]
    u_z1 = links.push(sgr.at[z1], gr.at[2], to_z1)
    gb1a = g1a(1, gb2b)
    u_z1.wait_recv()
    sgr[z] = sgr[z] + gr[2]
    u_y = links.push(sgr.at[z, 1 - yh], gc.at[0], to_y)
    gcy = gy(2, gc1b)
    gb1b = g1b(1, gb1a)
    u_y.wait_recv()
    gc[1] = sgr[z, yh] + gc[0]
    u_x1 = links.push(gc.at[1], gc.at[2], to_x1)
    ga1a = g1a(0, ga2b)
    u_x1.wait_recv()
    gc[3] = gc[1] + gc[2]
    u_x3 = links.push(gc.at[3], gc.at[4], to_x3)
    ga1b = g1b(0, ga1a)
    gby = gy(1, gb1b)
    u_x3.wait_recv()
    gc[5] = gc[3] + gc[4]
    u_far = links.push(gc.at[5], gc.at[6], to_far)
    sum_wait(2, o_second)

    def out_rows(i):
        r = i * 32
        bo_out[pl.ds(r, 32), :] = (mid[pl.ds(r, 32), :] + sum_rows(2, r, 32)).astype(BF16)

    loop(4, out_rows)
    u_far.wait_recv()
    gc[7] = gc[5] + gc[6]
    u_core = links.push(gc.at[7], gc.at[8], to_core)
    gay = gy(0, ga1b)
    gend(2, gcy)
    gend(1, gby)
    u_core.wait_recv()
    sg_out[...] = gc[7] + gc[8]
    gend(0, gay)
    for c in links.open:
        c.wait_send()


N_COPIES = 176


def train_call(lengths, tokens, cotangent, small_tile, mix_in, mix_out, gate_up, down):
    vmem = pl.BlockSpec(memory_space=pltpu.VMEM)
    rows = (2, 2, BLOCK)
    return pl.pallas_call(
        train_kernel,
        out_shape=(
            jax.ShapeDtypeStruct((BLOCK, D), BF16),
            jax.ShapeDtypeStruct((BLOCK, D), F32),
            jax.ShapeDtypeStruct((SHARD, WIDE), F32),
            jax.ShapeDtypeStruct((8, TILE), F32),
        ),
        in_specs=[pl.BlockSpec(memory_space=pltpu.SMEM)] + [vmem] * 7,
        out_specs=[vmem] * 4,
        scratch_shapes=[
            pltpu.VMEM((NZ, NY, NX, SHARD, WIDE), BF16),
            pltpu.VMEM((NZ, NY, NX, SHARD, WIDE), BF16),
            pltpu.VMEM(rows + (D,), BF16),
            pltpu.VMEM(rows + (D,), BF16),
            pltpu.VMEM(rows + (D,), BF16),
            pltpu.VMEM(rows + (D,), BF16),
            pltpu.VMEM(rows + (D,), BF16),
            pltpu.VMEM((2, ROWS, TILE), F32),
            pltpu.VMEM((3, ROWS, CH), F32),
            pltpu.VMEM((ROWS, CH), F32),
            pltpu.VMEM(rows + (CH,), BF16),
            pltpu.VMEM(rows + (3 * CH,), BF16),
            pltpu.VMEM((TILES, ROWS, CH), F32),
            pltpu.VMEM(rows + (HID,), BF16),
            pltpu.VMEM(rows + (2 * HID,), BF16),
            pltpu.VMEM((BLOCK, D), F32),
            pltpu.VMEM((BLOCK, D), F32),
            pltpu.VMEM((8, D), F32),
            pltpu.VMEM((4, 8, TILE), F32),
            pltpu.VMEM((4, 8, TILE), F32),
            pltpu.VMEM((NZ, NY, 8, TILE), F32),
            pltpu.VMEM((NZ, NY, 8, TILE), F32),
            pltpu.VMEM((3, NY, 8, TILE), F32),
            pltpu.VMEM((9, 8, TILE), F32),
            pltpu.VMEM((8, D), F32),
            pltpu.VMEM((4, NZ, 2, BLOCK, CH), BF16),
            pltpu.VMEM((4, NZ, 2, BLOCK, CH), BF16),
            pltpu.VMEM((4, NZ, 2, BLOCK, CH), F32),
            pltpu.VMEM((4, NZ, BLOCK, CH), BF16),
            pltpu.VMEM((4, NZ, BLOCK, CH), BF16),
            pltpu.VMEM((2, 2, 4, HALF, WIDE), BF16),
            pltpu.VMEM((2, NY, NX, HALF, WIDE), BF16),
            pltpu.VMEM((2, NZ, NY, HALF, WIDE), BF16),
            pltpu.VMEM((2, 2, HALF, WIDE), BF16),
            pltpu.VMEM((2, 2, 2, HALF, WIDE), BF16),
            pltpu.VMEM((SHARD, WIDE), BF16),
            pltpu.SemaphoreType.DMA((N_COPIES,)),
            pltpu.SemaphoreType.DMA((N_COPIES,)),
        ],
        compiler_params=pltpu.CompilerParams(
            collective_id=0, has_side_effects=True, vmem_limit_bytes=63 * 1024 * 1024
        ),
        cost_estimate=pl.CostEstimate(
            flops=6 * ROWS * D * WIDE, bytes_accessed=8 * 1024 * 1024, transcendentals=ROWS * HID
        ),
    )(lengths, tokens, cotangent, small_tile, mix_in, mix_out, gate_up, down)


def adam_step(weight, grad, first, second, rate):
    first_new = BETA_FIRST * first + (1.0 - BETA_FIRST) * grad
    second_new = BETA_SECOND * second + (1.0 - BETA_SECOND) * grad * grad
    first_hat = first_new / (1.0 - BETA_FIRST**STEP)
    second_hat = second_new / (1.0 - BETA_SECOND**STEP)
    weight_new = weight - rate * (
        first_hat / (jnp.sqrt(second_hat) + ADAM_EPSILON) + DECAY_RATE * weight
    )
    return (first_new, second_new, weight_new)


def adam_kernel(bo, tg, gs, sgrad, *refs):
    small, mix_in, mix_out, gate_up, down = refs[0:5]
    moments = refs[5:15]
    bo_new, tg_new = refs[15:17]
    outs = refs[17:]
    bo_new[...] = bo[...]
    tg_new[...] = tg[...]

    def put(k, where, grad, weight, rate):
        found = adam_step(weight[where], grad, moments[2 * k][where], moments[2 * k + 1][where], rate)
        for ref, value in zip(outs[3 * k : 3 * k + 3], found):
            ref[where] = value

    put(0, ..., sgrad[...], small, RATE_SMALL)
    for j in range(3):
        put(1, j, gs[:, j * CH : (j + 1) * CH], mix_in, RATE_PROJ)
    put(2, ..., gs[:, OUT_AT:GU_AT], mix_out, RATE_PROJ)
    for i in range(TILES):
        for j in range(2):
            lo = GU_AT + (2 * i + j) * TILE
            put(
                3,
                (j, slice(None), slice(i * TILE, (i + 1) * TILE)),
                gs[:, lo : lo + TILE],
                gate_up,
                RATE_PROJ,
            )
    put(4, ..., gs[:, DOWN_AT:WIDE], down, RATE_DOWN)


def per_device(
    tokens,
    cotangent,
    lengths,
    small,
    mix_in,
    mix_out,
    ffn_gate_up,
    ffn_down,
    small_first,
    small_second,
    in_first,
    in_second,
    out_first,
    out_second,
    gate_up_first,
    gate_up_second,
    down_first,
    down_second,
):
    place = ((lax.axis_index("dp") % 4) * 4 + lax.axis_index("tensor")) * 8
    tile = lax.dynamic_update_slice(jnp.zeros((8, TILE), F32), small, (0, place))
    bo, tg, gs, sg = train_call(
        lengths, tokens, cotangent, tile, mix_in, mix_out, ffn_gate_up, ffn_down
    )
    sgrad = lax.dynamic_slice(sg, (0, place), small.shape)
    weights = (small, mix_in, mix_out, ffn_gate_up, ffn_down)
    moments = (
        small_first,
        small_second,
        in_first,
        in_second,
        out_first,
        out_second,
        gate_up_first,
        gate_up_second,
        down_first,
        down_second,
    )
    out_shape = [jax.ShapeDtypeStruct(v.shape, v.dtype) for v in (bo, tg)]
    for v in weights:
        out_shape += [jax.ShapeDtypeStruct(v.shape, v.dtype)] * 3
    vmem = pl.BlockSpec(memory_space=pltpu.VMEM)
    return tuple(
        pl.pallas_call(
            adam_kernel,
            out_shape=out_shape,
            in_specs=[vmem] * 19,
            out_specs=[vmem] * 17,
            compiler_params=pltpu.CompilerParams(vmem_limit_bytes=32 * 1024 * 1024),
        )(bo, tg, gs, sgrad, *weights, *moments)
    )


def solution(mesh):
    rows = P(("dp", "tensor"), None)
    small = P(None, ("dp", "tensor"))
    deep = P(None, "dp", "tensor")
    flat = P("dp", "tensor")
    in_specs = (rows, rows, P("dp", None), small, deep, flat, deep, flat)
    in_specs += (small,) * 2 + (deep,) * 2 + (flat,) * 2 + (deep,) * 2 + (flat,) * 2
    out_specs = (rows, rows) + (small,) * 3 + (deep,) * 3 + (flat,) * 3 + (deep,) * 3 + (flat,) * 3
    return jax.shard_map(
        per_device, mesh=mesh, in_specs=in_specs, out_specs=out_specs, check_vma=False
    )
```

time: 1430 us -> 175 us (0.12)
  waiting for transfers between devices: 977 us -> 0 us
  blocking collectives: 339 us -> 0 us
  Pallas kernels: 0 us -> 160 us
  matrix products: 46.9 us -> 0 us
  other arithmetic: 27.1 us -> 0 us
  between operations: 15.2 us -> 0.77 us
    reduce_scatter x6 -> x0, waiting for transfers between devices: 426 us -> none  [the longest x1 225 us: per_device(): lax.psum_scatter(down_grad.astype(jnp.bfloat16), 'dp', scatter_dimension=...]
    unnamed x15 -> x0, waiting for transfers between devices: 335 us -> none
    all_gather x2 -> x0, blocking collectives: 271 us -> none  [the longest x1 180 us: per_device(): small_all = lax.all_gather(small, ('dp', 'tensor'), axis=1, tiled=True)]
    all_gather x7 -> x0, waiting for transfers between devices: 216 us -> none  [the longest x1 88.3 us: per_device(): lax.all_gather(ffn_gate_up.astype(jnp.bfloat16), 'dp', axis=1, tiled=True)]
    pallas_call x0 -> x2, Pallas kernels: none -> 160 us  [the longest x1 158 us: train_call(): pl.pallas_call(train_kernel, out_shape=(jax.ShapeDtypeStruct((BLOCK, D),...]
    unnamed x1 -> x0, blocking collectives: 68.4 us -> none
    dot_general x12 -> x0, matrix products: 46.9 us -> none  [the longest x1 7.43 us: per_device(): jnp.einsum('rd,jdf->jrf', rows_two, gu_w, preferred_element_type=jnp.floa...]
    convert_element_type x2 -> x0, local copies, waits for them, and re-layouts: 15.2 us -> none  [the longest x1 12.6 us: per_device(): gate_up_grad.astype(jnp.bfloat16)]
  transfers between devices with their start and end apart: 14 -> 0, of which waited for: 11 -> 0; matrix products, arithmetic and copies ran while one was open for 4% -> 0% of each run, Pallas kernels for 0% -> 0%
where the time goes in v1:
time: 175 us; the launch traced here: 174 us
  Pallas kernels  160 us (91%)
  local copies, waits for them, and re-layouts  13.2 us (8%)
    pallas_call x1, Pallas kernels, train_call(): pl.pallas_call(train_kernel, out_shape=(jax.ShapeDtypeStruct((BLOCK, D),...  158 us
    unnamed x40, local copies, waits for them, and re-layouts  11.2 us

profile of v1, /device:TPU:0, one launch (start us, length us, event | category | flops | bytes accessed | tf_op | source)
XLA Modules:
  0.0 173.9 jit_solution(7296301075928178559)
XLA Ops:
  0.7 0.0 copy-start.15
  0.7 0.6 broadcast_in_dim.3
  1.3 0.1 copy-done.15
  1.4 1.4 dynamic_update_slice.3.small_in
  2.7 0.0 copy-start.2
  2.7 0.0 copy-start.3
  2.7 0.0 copy-start.4
  2.8 0.0 copy-start.9
  2.8 158.2 %shard_map.305 = (bf16[128,1024]{1,0:T(8,128)(2,1)}, f32[128,1024]{1,0:T(8,128)}, f32[32,4480]{1,0:T(8,128)}, f32[8,128]{1,0:T(8,128)}) custom-call(s32[1,4]{1,0:T(1,128)} %lens.1, bf16[128,1024]{1,0:T(8,128)(2,1)} %tok_in.1, bf16[128,1024]{1,0:T(8,128)(2,1)} %cot_in.1, f32[8,128]{1,0:T(8,128)} %dynamic_update_slice.3.small_in, f32[3,32,256]{2,1,0:T(8,128)} %refs_1_.1, ...), custom_call_target="tpu_custom_call" | custom-call | flops 14092861440 | bytes 8388608 | tf_op jit(solution)/shard_map/pallas_call | solution.py:640
  160.9 0.0 copy-start.19
  160.9 0.0 copy-start.18
  161.0 0.7 copy-done.19
  161.6 0.0 copy-start.16
  161.6 0.0 copy-start.17
  161.6 0.1 constant_dynamic-slice_fusion.sgrad
  161.7 0.0 copy-done.2
  161.7 0.0 copy-done.3
  161.7 0.0 copy-done.4
  161.7 0.0 copy-done.9
  161.7 0.0 copy-done.18
  161.7 0.6 copy-done.16
  162.3 0.0 copy-done.17
  162.3 0.0 copy-start
  162.3 1.1 copy-done
  163.4 0.0 copy-start.1
  163.4 1.0 copy-done.1
  164.4 0.0 copy-start.5
  164.4 0.9 copy-done.5
  165.4 0.0 copy-start.6
  165.4 0.9 copy-done.6
  166.3 0.0 copy-start.7
  166.3 0.9 copy-done.7
  167.2 0.0 copy-start.8
  167.2 0.9 copy-done.8
  168.1 0.0 copy-start.10
  168.1 0.9 copy-done.10
  169.0 0.0 copy-start.11
  169.0 0.9 copy-done.11
  169.9 0.0 copy-start.12
  169.9 0.8 copy-done.12
  170.6 0.0 copy-start.13
  170.6 0.8 copy-done.13
  171.4 0.0 copy-start.14
  171.4 0.8 copy-done.14
  172.2 1.8 %shard_map.306 = (bf16[128,1024]{1,0:T(8,128)(2,1)}, f32[128,1024]{1,0:T(8,128)}, f32[5,8]{1,0:T(8,128)}, f32[5,8]{1,0:T(8,128)}, f32[5,8]{1,0:T(8,128)}, /*inde...) custom-call(bf16[128,1024]{1,0:T(8,128)(2,1)S(1)} %copy-done.5, ...), custom_call_target="tpu_custom_call" | custom-call | tf_op jit(solution)/shard_map/pallas_call | solution.py:784
Async XLA Ops:
  0.7 0.7 copy-start.15
  2.7 159.0 %copy-start.2 = (f32[2,32,1152]{2,1,0:T(8,128)S(1)}, f32[2,32,1152]{2,1,0:T(8,128)}, u32[]{:S(2)}) copy-start(f32[2,32,1152]{2,1,0:T(8,128)} %refs_3_.1) | copy-start | bytes 884740
  2.7 159.0 %copy-start.3 = (f32[2,32,1152]{2,1,0:T(8,128)S(1)}, f32[2,32,1152]{2,1,0:T(8,128)}, u32[]{:S(2)}) copy-start(f32[2,32,1152]{2,1,0:T(8,128)} %refs_11_.1) | copy-start | bytes 884740
  2.7 158.9 %copy-start.4 = (f32[2,32,1152]{2,1,0:T(8,128)S(1)}, f32[2,32,1152]{2,1,0:T(8,128)}, u32[]{:S(2)}) copy-start(f32[2,32,1152]{2,1,0:T(8,128)} %refs_12_.1) | copy-start | bytes 884740
  2.8 158.9 %copy-start.9 = (f32[3,32,256]{2,1,0:T(8,128)S(1)}, f32[3,32,256]{2,1,0:T(8,128)}, u32[]{:S(2)}) copy-start(f32[3,32,256]{2,1,0:T(8,128)} %refs_1_.1) | copy-start | bytes 294916
  160.9 0.7 copy-start.19
  160.9 0.8 copy-start.18
  161.6 0.7 copy-start.16
  161.6 0.7 copy-start.17
  162.3 1.1 copy-start
  163.4 1.0 copy-start.1
  164.4 0.9 copy-start.5
  165.4 0.9 copy-start.6
  166.3 0.9 copy-start.7
  167.2 0.9 copy-start.8
  168.1 0.9 copy-start.10
  169.0 0.9 copy-start.11
  169.9 0.8 copy-start.12
  170.6 0.8 copy-start.13
  171.4 0.8 copy-start.14

commit v2 on v1

--- a/solution.py
+++ b/solution.py
@@ -32,7 +32,14 @@
 GU_AT = 4 * CH
 DOWN_AT = GU_AT + 2 * HID
 WIDE = DOWN_AT + HID
-PARTS = ((0, GU_AT), (GU_AT, 2 * HID), (DOWN_AT, HID))
+FIRST = TILES // 2
+GU_PARTS = ((0, FIRST), (FIRST, TILES - FIRST))
+PARTS = (
+    (0, GU_AT),
+    (GU_AT, FIRST * CH),
+    (GU_AT + FIRST * CH, (TILES - FIRST) * CH),
+    (DOWN_AT, HID),
+)
 NZ, NY, NX, SHARD = 4, 2, 4, 32
 HALF = SHARD // 2
 
@@ -51,6 +58,17 @@
 
 def at_lane(i, width):
     return pl.ds(pl.multiple_of(i * width, width), width)
+
+
+def adam_step(weight, grad, first, second, rate):
+    first_new = BETA_FIRST * first + (1.0 - BETA_FIRST) * grad
+    second_new = BETA_SECOND * second + (1.0 - BETA_SECOND) * grad * grad
+    first_hat = first_new / (1.0 - BETA_FIRST**STEP)
+    second_hat = second_new / (1.0 - BETA_SECOND**STEP)
+    weight_new = weight - rate * (
+        first_hat / (jnp.sqrt(second_hat) + ADAM_EPSILON) + DECAY_RATE * weight
+    )
+    return (first_new, second_new, weight_new)
 
 
 class Links:
@@ -84,19 +102,30 @@
         c.wait_recv()
 
 
-def train_kernel(
+def train_kernel(*refs):
+    lens, tok_in, cot_in = refs[:3]
+    state_in = refs[3:18]
+    bo_out, tg_out = refs[18:20]
+    state_out = refs[20:35]
+    train_body(lens, tok_in, cot_in, state_in, bo_out, tg_out, state_out, *refs[35:])
+
+
+def train_body(
     lens,
     tok_in,
     cot_in,
-    small_in,
-    win,
-    wout,
-    wgu,
-    wdn,
+    state_in,
     bo_out,
     tg_out,
-    gs_out,
-    sg_out,
+    state_out,
+    state_small,
+    state_in_w,
+    state_out_w,
+    state_gu,
+    state_down,
+    bo,
+    tg,
+    local_sem,
     w,
     g,
     tok,
@@ -122,6 +151,7 @@
     gr,
     gc,
     gacc,
+    invs,
     ps,
     pr,
     po,
@@ -149,24 +179,34 @@
     to_y = at(z, 1 - yh, x)
     to_xp, to_xm = at(z, yh, xp), at(z, yh, xm)
     to_zp, to_zm = at(zp, yh, x), at(zm, yh, x)
-    x1 = x + 1 - 2 * (x % 2)
-    z1 = z + 1 - 2 * (z % 2)
-    to_x1, to_x3 = at(z, yh, x1), at(z, yh, 3 - x)
-    to_z1, to_z3 = at(z1, yh, x), at(3 - z, yh, x)
+    to_xo, to_zo = at(z, yh, xo), at(zo, yh, x)
     to_core = (dp, ty * 2 + 1 - tc)
     to_far = (dp, (1 - ty) * 2 + tc)
+    to_across = (dp, (1 - ty) * 2 + 1 - tc)
     links = Links(send_sem, recv_sem)
 
-    for j in range(3):
-        w[z, yh, x, :, j * CH : (j + 1) * CH] = win[j].astype(BF16)
-    w[z, yh, x, :, OUT_AT : OUT_AT + CH] = wout[...].astype(BF16)
-    for i in range(TILES):
-        for j in range(2):
-            lo = GU_AT + (2 * i + j) * TILE
-            w[z, yh, x, :, lo : lo + TILE] = wgu[j, :, i * TILE : (i + 1) * TILE].astype(BF16)
-    w[z, yh, x, :, DOWN_AT:WIDE] = wdn[...].astype(BF16)
-    tok[ty, tc] = tok_in[...]
-    st[0] = small_in[...]
+    barrier = pltpu.get_barrier_semaphore()
+    peers = (to_y, to_xp, to_xm, to_xo, to_zp, to_zm, to_zo, to_core, to_far, to_across)
+    for to in peers:
+        pl.semaphore_signal(barrier, inc=1, device_id=to, device_id_type=MESH)
+
+    state = (state_small, state_in_w, state_out_w, state_gu, state_down)
+    n_local = 0
+    loads = {}
+    for key, src, dst in (
+        [((k, 0), state_in[k], state[k].at[0]) for k in range(5)]
+        + [("tok", tok_in, tok.at[ty, tc]), ("cot", cot_in, cot.at[ty, tc])]
+        + [((k, j), state_in[3 + 2 * k + j + 1], state[k].at[j]) for k in range(5) for j in (1, 2)]
+    ):
+        loads[key] = pltpu.make_async_copy(src, dst, local_sem.at[n_local])
+        loads[key].start()
+        n_local += 1
+    stores = []
+
+    def store(src, dst):
+        c = pltpu.make_async_copy(src, dst, local_sem.at[n_local + len(stores)])
+        c.start()
+        stores.append(c)
 
     row = lax.broadcasted_iota(jnp.int32, (ROWS, TILE), 0)
     start = jnp.zeros((ROWS, TILE), jnp.int32)
@@ -177,13 +217,18 @@
     dist = row - start
     masks[0] = jnp.where(dist >= 1, 1.0, 0.0)
     masks[1] = jnp.where(dist >= 2, 1.0, 0.0)
-    my_row = lax.broadcasted_iota(jnp.int32, (BLOCK, D), 0) + t * BLOCK
-    cot[ty, tc] = jnp.where(my_row < run, cot_in[...].astype(F32), 0.0).astype(BF16)
-
-    barrier = pltpu.get_barrier_semaphore()
-    peers = (to_y, to_xp, to_xm, to_zp, to_zm, to_core, to_far)
-    for to in peers:
-        pl.semaphore_signal(barrier, inc=1, device_id=to, device_id_type=MESH)
+
+    place = ((dp % 4) * 4 + t) * 8
+    st[0] = jnp.zeros((8, TILE), F32)
+    loads[0, 0].wait()
+    st[0, 0:5, 0:8] = state_small[0]
+    st[0] = pltpu.roll(st[0], place, 1)
+    loads[1, 0].wait()
+    for j in range(3):
+        w[z, yh, x, :, j * CH : (j + 1) * CH] = state_in_w[0, j].astype(BF16)
+    loads[2, 0].wait()
+    w[z, yh, x, :, OUT_AT : OUT_AT + CH] = state_out_w[0].astype(BF16)
+    loads["tok"].wait()
     pl.semaphore_wait(barrier, len(peers))
 
     lo_half, hi_half = pl.ds(0, HALF), pl.ds(HALF, HALF)
@@ -354,47 +399,93 @@
             )
         return links.push(g.at[z, 1 - yh, x, :, c], ry.at[:, c], to_y)
 
+    def update(k, where, grad, rate):
+        ref = state[k]
+        found = adam_step(ref[(0, *where)], grad, ref[(1, *where)], ref[(2, *where)], rate)
+        for j, value in enumerate(found):
+            ref[((1, 2, 0)[j], *where)] = value
+
+    def put(k):
+        for j in range(3):
+            store(state[k].at[(1, 2, 0)[j]], state_out[3 * k + j])
+
+    def total(lo, n):
+        return g[z, yh, x, :, lo : lo + n].astype(F32) + ry[:, lo : lo + n].astype(F32)
+
     def gend(p, copy):
-        c = cols(p)
         copy.wait_recv()
-        gs_out[:, c] = g[z, yh, x, :, c].astype(F32) + ry[:, c].astype(F32)
-
-    s_far = links.push(st.at[0], sr.at[0], to_far)
-    y0 = wy(0)
+        if p == 0:
+            for k in (1, 2):
+                for j in (1, 2):
+                    loads[k, j].wait()
+            for j in range(3):
+                update(1, (j,), total(j * CH, CH), RATE_PROJ)
+            update(2, (), total(OUT_AT, CH), RATE_PROJ)
+            put(1)
+            put(2)
+        elif p < 3:
+            if p == 1:
+                for j in (1, 2):
+                    loads[3, j].wait()
+            first, n = GU_PARTS[p - 1]
+            for i in range(first, first + n):
+                for j in range(2):
+                    where = (j, slice(None), slice(i * TILE, (i + 1) * TILE))
+                    update(3, where, total(GU_AT + (2 * i + j) * TILE, TILE), RATE_PROJ)
+            if p == 2:
+                put(3)
+        else:
+            for j in (1, 2):
+                loads[4, j].wait()
+            update(4, (), total(DOWN_AT, HID), RATE_DOWN)
+            put(4)
+
+    tensor_peers = (to_core, to_far, to_across)
+    x_peers = (to_xp, to_xo, to_xm)
+    z_peers = (to_zp, to_zo, to_zm)
+
+    def tile_send(src, slots, first, to_all):
+        return [links.push(src, slots.at[first + i], to) for i, to in enumerate(to_all)]
+
+    def tile_sum(own, slots, first, copies):
+        arrived(copies)
+        return own + slots[first] + slots[first + 1] + slots[first + 2]
+
+    s_t = tile_send(st.at[0], sr, 0, tensor_peers)
+    ya = wy(0)
     tok_c = rows_start(tok)
-    y1 = wy(1)
-    y2 = wy(2)
-    s_far.wait_recv()
-    st[1] = st[0] + sr[0]
-    s_core = links.push(st.at[1], sr.at[1], to_core)
-    y0.wait_recv()
-    a1a = w1a(0)
-    s_core.wait_recv()
-    st[2] = st[1] + sr[1]
-    s_x1 = links.push(st.at[2], sr.at[2], to_x1)
+    loads[3, 0].wait()
+    for i in range(TILES):
+        for j in range(2):
+            lo = GU_AT + (2 * i + j) * TILE
+            w[z, yh, x, :, lo : lo + TILE] = state_gu[0, j, :, i * TILE : (i + 1) * TILE].astype(BF16)
+    yb = wy(1)
+    ye = wy(2)
+    loads[4, 0].wait()
+    w[z, yh, x, :, DOWN_AT:WIDE] = state_down[0].astype(BF16)
+    yc = wy(3)
+    st[1] = tile_sum(st[0], sr, 0, s_t)
+    s_x = tile_send(st.at[1], sr, 3, x_peers)
+    ya.wait_recv()
+    a1 = w1a(0)
+    sm[z, yh] = tile_sum(st[1], sr, 3, s_x)
+    s_y = same(sm.at[z, yh], to_y)
+    arrived(a1)
+    a1 = w1b(0)
+    yb.wait_recv()
+    b1 = w1a(1)
+    s_y.wait_recv()
+    s_z = [same(sm.at[z], to) for to in z_peers]
+    arrived(a1)
+    a2 = w2a(0)
     rows_relay(tok, tok_c)
-    arrived(a1a)
-    a1b = w1b(0)
-    s_x1.wait_recv()
-    st[3] = st[2] + sr[2]
-    s_x3 = links.push(st.at[3], sr.at[3], to_x3)
-    y1.wait_recv()
-    b1a = w1a(1)
-    s_x3.wait_recv()
-    sm[z, yh] = st[3] + sr[3]
-    s_y = same(sm.at[z, yh], to_y)
-    arrived(a1b)
-    a2a = w2a(0)
-    y2.wait_recv()
-    c1a = w1a(2)
-    s_y.wait_recv()
-    s_z1 = same(sm.at[z], to_z1)
-    cot_c = rows_start(cot)
-    s_z1.wait_recv()
-    s_z3 = same(sm.at[pl.ds((z // 2) * 2, 2)], to_z3)
-    arrived(b1a)
-    b1b = w1b(1)
-    s_z3.wait_recv()
+    ye.wait_recv()
+    e1 = w1a(2)
+    arrived(b1)
+    b1 = w1b(1)
+    yc.wait_recv()
+    c1 = w1a(3)
+    arrived(s_z)
     for k in range(8):
         sml[:, k * TILE : (k + 1) * TILE] = sm[k // 2, k % 2]
     rows_wait(tok_c)
@@ -404,23 +495,32 @@
         v = tok[a, b, pl.ds(r, 32), :].astype(F32)
         inv = lax.rsqrt(jnp.mean(v * v, axis=1, keepdims=True) + NORM_EPSILON)
         one[a, b, pl.ds(r, 32), :] = (v * inv * sml[0:1, :]).astype(BF16)
+        invs[a, b, pl.ds(r, 32), :] = jnp.broadcast_to(inv, (32, TILE))
 
     loop(16, norm_in)
-    arrived(a2a)
-    a2b = w2b(0)
-    arrived(b1b)
-    b2a = w2a(1)
-    arrived(c1a)
-    c1b = w1b(2)
-    rows_relay(cot, cot_c)
-    arrived(a2b)
+    arrived(e1)
+    e1 = w1b(2)
+    arrived(b1)
+    arrived(a2)
+    a2 = w2b(0)
+    b2 = w2a(1)
+    arrived(c1)
+    c1 = w1b(3)
+    loads["cot"].wait()
+    my_row = lax.broadcasted_iota(jnp.int32, (32, D), 0) + t * BLOCK
+
+    def mask_rows(i):
+        v = cot[ty, tc, pl.ds(i * 32, 32), :].astype(F32)
+        cot[ty, tc, pl.ds(i * 32, 32), :] = jnp.where(my_row + i * 32 < run, v, 0.0).astype(BF16)
+
+    loop(4, mask_rows)
+    cot_c = rows_start(cot)
+    arrived(a2)
 
     def proj(j):
         pj[j] = mm(one[...].reshape(ROWS, D), w[:, :, :, :, at_lane(j, CH)].reshape(D, CH))
 
     loop(3, proj)
-    arrived(c1b)
-    c2a = w2a(2)
 
     def taps(k, lanes):
         return sml[2 + k : 3 + k, lanes]
@@ -436,6 +536,10 @@
         gated[:, :, :, lanes] = (pj[1, :, lanes] * v).astype(BF16).reshape(2, 2, BLOCK, TILE)
 
     m_first = sum_start(0, gated, OUT_AT, CH)
+    arrived(b2)
+    b2 = w2b(1)
+    arrived(e1)
+    e2 = w2a(2)
     m_second = sum_cross(0, m_first)
     sum_wait(0, m_second)
 
@@ -448,12 +552,14 @@
 
     loop(4, norm_mid)
     two_c = rows_start(two)
-    arrived(b2a)
-    b2b = w2b(1)
+    rows_relay(cot, cot_c)
+    arrived(e2)
+    e2 = w2b(2)
+    arrived(c1)
+    c2 = w2a(3)
     rows_relay(two, two_c)
     rows_wait(two_c)
-    rows_wait(cot_c)
-    arrived(b2b)
+    arrived(b2)
 
     def gate_up(i):
         lanes = pl.ds(pl.multiple_of(GU_AT + i * CH, CH), CH)
@@ -465,9 +571,12 @@
         gu[i, :, :TILE] = up * s * (1.0 + gate * (1.0 - s))
         gu[i, :, TILE:] = act
 
-    loop(TILES, gate_up)
-    arrived(c2a)
-    c2b = w2b(2)
+    loop(FIRST, gate_up)
+    arrived(e2)
+    loop(TILES - FIRST, lambda i: gate_up(i + FIRST))
+    arrived(c2)
+    c2 = w2b(3)
+    rows_wait(cot_c)
 
     def wide(v):
         return v.reshape(NY, NX, SHARD, v.shape[1])
@@ -477,8 +586,8 @@
         g[i, :, :, :, DOWN_AT:WIDE] = wide(mm(a, hid[...].reshape(ROWS, HID)).astype(BF16))
 
     loop(NZ, down_grad)
-    gc2a = g2a(2)
-    arrived(c2b)
+    gc_ = g2a(3)
+    arrived(c2)
 
     def back_tile(k, gh):
         v = gu[k]
@@ -493,23 +602,31 @@
         back_tile(2 * i, v[:, :TILE])
         back_tile(2 * i + 1, v[:, TILE:])
 
+    def gate_up_grad(p):
+        first, n = GU_PARTS[p - 1]
+
+        def step(i):
+            a = two[:, :, :, at_lane(i, CH)].reshape(ROWS, CH).T
+            b = gg[:, :, :, first * CH : (first + n) * CH].reshape(ROWS, n * CH)
+            lo = GU_AT + first * CH
+            g[i, :, :, :, lo : lo + n * CH] = wide(mm(a, b).astype(BF16))
+
+        loop(NZ, step)
+
     loop(TILES // 2, grad_hidden)
     back_tile(
         TILES - 1,
         mm(cot[...].reshape(ROWS, D), w[:, :, :, :, WIDE - TILE : WIDE].reshape(D, TILE)),
     )
+    gc_ = g2b(3, gc_)
+    gate_up_grad(1)
+    gb_ = g2a(1)
     n_first = sum_start(1, gg, GU_AT, 2 * HID)
+    gate_up_grad(2)
+    ge_ = g2a(2)
     n_second = sum_cross(1, n_first)
-
-    def gate_up_grad(i):
-        a = two[:, :, :, at_lane(i, CH)].reshape(ROWS, CH).T
-        for q in range(3):
-            lo = q * 3 * CH
-            b = gg[:, :, :, lo : lo + 3 * CH].reshape(ROWS, 3 * CH)
-            g[i, :, :, :, GU_AT + lo : GU_AT + lo + 3 * CH] = wide(mm(a, b).astype(BF16))
-
-    loop(NZ, gate_up_grad)
-    gb2a = g2a(1)
+    gc_ = g1a(3, gc_)
+    gb_ = g2b(1, gb_)
     sum_wait(1, n_second)
     gacc[...] = jnp.zeros_like(gacc)
 
@@ -528,15 +645,14 @@
 
     loop(4, norm_two_back)
     mid_c = rows_start(rmid)
-    gc2b = g2b(2, gc2a)
+    o_first = sum_start(2, hid, DOWN_AT, HID)
+    ge_ = g2b(2, ge_)
+    gc_ = g1b(3, gc_)
     rows_relay(rmid, mid_c)
-    o_first = sum_start(2, hid, DOWN_AT, HID)
+    o_second = sum_cross(2, o_first)
     rows_wait(mid_c)
-    gc1a = g1a(2, gc2b)
-    gb2b = g2b(1, gb2a)
-
-    pj_c = mm(rmid[...].reshape(ROWS, D), w[:, :, :, :, OUT_AT : OUT_AT + CH].reshape(D, CH))
-    pg = pj_c
+
+    pg = mm(rmid[...].reshape(ROWS, D), w[:, :, :, :, OUT_AT : OUT_AT + CH].reshape(D, CH))
     for q in range(2):
         lanes = slice(q * TILE, (q + 1) * TILE)
         own = at_lane(t * 2 + q, TILE)
@@ -567,87 +683,101 @@
         g[i, :, :, :, OUT_AT:GU_AT] = wide(mm(b, gated[...].reshape(ROWS, CH)).astype(BF16))
 
     loop(NZ, mix_grad)
-    ga2a = g2a(0)
+    ga_ = g2a(0)
+
+    def gain_one(i):
+        lanes = at_lane(i, CH)
+        out = jnp.zeros((1, CH), F32)
+        for c, terms in ((1 - tc, ps), (tc, po)):
+            for a in range(2):
+                unit = tok[a, c, :, lanes].astype(F32) * jnp.tile(invs[a, c], (1, 2))
+                out += jnp.sum(terms[3, i, a].astype(F32) * unit, axis=0, keepdims=True)
+        gacc[0:1, lanes] = out
+
+    loop(NZ, gain_one)
+    for k in range(8):
+        sgr[k // 2, k % 2] = gacc[:, k * TILE : (k + 1) * TILE]
+    u_z = [
+        links.push(sgr.at[zz], gr.at[i], to)
+        for i, (zz, to) in enumerate(((zp, to_zp), (zo, to_zo), (zm, to_zm)))
+    ]
     i_second = sum_cross(3, i_first)
-    gc1b = g1b(2, gc1a)
-    o_second = sum_cross(2, o_first)
+    gb_ = g1a(1, gb_)
+    gc_ = gy(3, gc_)
+    arrived(u_z)
+    sgr[z] = sgr[z] + gr[0] + gr[1] + gr[2]
+    u_y = links.push(sgr.at[z, 1 - yh], gc.at[0], to_y)
+    ge_ = g1a(2, ge_)
+    ga_ = g2b(0, ga_)
+    gb_ = g1b(1, gb_)
+    u_y.wait_recv()
+    gc[1] = sgr[z, yh] + gc[0]
+    u_x = tile_send(gc.at[1], gc, 2, x_peers)
+    sum_wait(2, o_second)
+
+    def out_rows(i):
+        r = i * 32
+        bo[pl.ds(r, 32), :] = (mid[pl.ds(r, 32), :] + sum_rows(2, r, 32)).astype(BF16)
+
+    loop(4, out_rows)
+    store(bo, bo_out)
+    ge_ = g1b(2, ge_)
+    gb_ = gy(1, gb_)
+    gend(3, gc_)
+    gc[5] = tile_sum(gc[1], gc, 2, u_x)
+    u_t = tile_send(gc.at[5], gc, 6, tensor_peers)
     sum_wait(3, i_second)
 
     def norm_one_back(i):
         r = i * 32
         gn = sum_rows(3, r, 32)
-        v = tok[ty, tc, pl.ds(r, 32), :].astype(F32)
-        inv = lax.rsqrt(jnp.mean(v * v, axis=1, keepdims=True) + NORM_EPSILON)
-        unit = v * inv
-        gacc[0:1, :] += jnp.sum(gn * unit, axis=0, keepdims=True)
+        unit = tok[ty, tc, pl.ds(r, 32), :].astype(F32)
+        inv = lax.rsqrt(jnp.mean(unit * unit, axis=1, keepdims=True) + NORM_EPSILON)
+        unit = unit * inv
         scaled = gn * sml[0:1, :]
         inner = jnp.mean(scaled * unit, axis=1, keepdims=True)
-        tg_out[pl.ds(r, 32), :] = gmid[pl.ds(r, 32), :] + inv * (scaled - unit * inner)
+        tg[pl.ds(r, 32), :] = gmid[pl.ds(r, 32), :] + inv * (scaled - unit * inner)
 
     loop(4, norm_one_back)
-    for k in range(8):
-        sgr[k // 2, k % 2] = gacc[:, k * TILE : (k + 1) * TILE]
-    pair = (z // 2) * 2
-    u_z3 = links.push(sgr.at[pl.ds(2 - pair, 2)], gr.at[pl.ds(0, 2)], to_z3)
-    ga2b = g2b(0, ga2a)
-    u_z3.wait_recv()
-    sgr[pl.ds(pair, 2)] = sgr[pl.ds(pair, 2)] + gr[0:2]
-    u_z1 = links.push(sgr.at[z1], gr.at[2], to_z1)
-    gb1a = g1a(1, gb2b)
-    u_z1.wait_recv()
-    sgr[z] = sgr[z] + gr[2]
-    u_y = links.push(sgr.at[z, 1 - yh], gc.at[0], to_y)
-    gcy = gy(2, gc1b)
-    gb1b = g1b(1, gb1a)
-    u_y.wait_recv()
-    gc[1] = sgr[z, yh] + gc[0]
-    u_x1 = links.push(gc.at[1], gc.at[2], to_x1)
-    ga1a = g1a(0, ga2b)
-    u_x1.wait_recv()
-    gc[3] = gc[1] + gc[2]
-    u_x3 = links.push(gc.at[3], gc.at[4], to_x3)
-    ga1b = g1b(0, ga1a)
-    gby = gy(1, gb1b)
-    u_x3.wait_recv()
-    gc[5] = gc[3] + gc[4]
-    u_far = links.push(gc.at[5], gc.at[6], to_far)
-    sum_wait(2, o_second)
-
-    def out_rows(i):
-        r = i * 32
-        bo_out[pl.ds(r, 32), :] = (mid[pl.ds(r, 32), :] + sum_rows(2, r, 32)).astype(BF16)
-
-    loop(4, out_rows)
-    u_far.wait_recv()
-    gc[7] = gc[5] + gc[6]
-    u_core = links.push(gc.at[7], gc.at[8], to_core)
-    gay = gy(0, ga1b)
-    gend(2, gcy)
-    gend(1, gby)
-    u_core.wait_recv()
-    sg_out[...] = gc[7] + gc[8]
-    gend(0, gay)
+    store(tg, tg_out)
+    ge_ = gy(2, ge_)
+    gend(1, gb_)
+    ga_ = g1a(0, ga_)
+    gc[9] = pltpu.roll(tile_sum(gc[5], gc, 6, u_t), TILE - place, 1)
+    for j in (1, 2):
+        loads[0, j].wait()
+    update(0, (), gc[9, 0:5, 0:8], RATE_SMALL)
+    put(0)
+    gend(2, ge_)
+    ga_ = g1b(0, ga_)
+    ga_ = gy(0, ga_)
+    gend(0, ga_)
     for c in links.open:
         c.wait_send()
-
-
-N_COPIES = 176
-
-
-def train_call(lengths, tokens, cotangent, small_tile, mix_in, mix_out, gate_up, down):
-    vmem = pl.BlockSpec(memory_space=pltpu.VMEM)
+    for c in stores:
+        c.wait()
+
+
+N_COPIES = 220
+
+
+def train_call(lengths, tokens, cotangent, *state):
+    anywhere = pl.BlockSpec(memory_space=pltpu.HBM)
     rows = (2, 2, BLOCK)
+    weights = state[:5]
+    out_shape = [jax.ShapeDtypeStruct((BLOCK, D), BF16), jax.ShapeDtypeStruct((BLOCK, D), F32)]
+    for v in weights:
+        out_shape += [jax.ShapeDtypeStruct(v.shape, F32)] * 3
     return pl.pallas_call(
         train_kernel,
-        out_shape=(
-            jax.ShapeDtypeStruct((BLOCK, D), BF16),
-            jax.ShapeDtypeStruct((BLOCK, D), F32),
-            jax.ShapeDtypeStruct((SHARD, WIDE), F32),
-            jax.ShapeDtypeStruct((8, TILE), F32),
-        ),
-        in_specs=[pl.BlockSpec(memory_space=pltpu.SMEM)] + [vmem] * 7,
-        out_specs=[vmem] * 4,
-        scratch_shapes=[
+        out_shape=out_shape,
+        in_specs=[pl.BlockSpec(memory_space=pltpu.SMEM)] + [anywhere] * 17,
+        out_specs=[anywhere] * 17,
+        scratch_shapes=[pltpu.VMEM((3,) + v.shape, F32) for v in weights]
+        + [
+            pltpu.VMEM((BLOCK, D), BF16),
+            pltpu.VMEM((BLOCK, D), F32),
+            pltpu.SemaphoreType.DMA((40,)),
             pltpu.VMEM((NZ, NY, NX, SHARD, WIDE), BF16),
             pltpu.VMEM((NZ, NY, NX, SHARD, WIDE), BF16),
             pltpu.VMEM(rows + (D,), BF16),
@@ -666,13 +796,14 @@
             pltpu.VMEM((BLOCK, D), F32),
             pltpu.VMEM((BLOCK, D), F32),
             pltpu.VMEM((8, D), F32),
-            pltpu.VMEM((4, 8, TILE), F32),
-            pltpu.VMEM((4, 8, TILE), F32),
+            pltpu.VMEM((2, 8, TILE), F32),
+            pltpu.VMEM((6, 8, TILE), F32),
             pltpu.VMEM((NZ, NY, 8, TILE), F32),
             pltpu.VMEM((NZ, NY, 8, TILE), F32),
             pltpu.VMEM((3, NY, 8, TILE), F32),
-            pltpu.VMEM((9, 8, TILE), F32),
+            pltpu.VMEM((10, 8, TILE), F32),
             pltpu.VMEM((8, D), F32),
+            pltpu.VMEM(rows + (TILE,), F32),
             pltpu.VMEM((4, NZ, 2, BLOCK, CH), BF16),
             pltpu.VMEM((4, NZ, 2, BLOCK, CH), BF16),
             pltpu.VMEM((4, NZ, 2, BLOCK, CH), F32),
@@ -693,48 +824,22 @@
         cost_estimate=pl.CostEstimate(
             flops=6 * ROWS * D * WIDE, bytes_accessed=8 * 1024 * 1024, transcendentals=ROWS * HID
         ),
-    )(lengths, tokens, cotangent, small_tile, mix_in, mix_out, gate_up, down)
-
-
-def adam_step(weight, grad, first, second, rate):
-    first_new = BETA_FIRST * first + (1.0 - BETA_FIRST) * grad
-    second_new = BETA_SECOND * second + (1.0 - BETA_SECOND) * grad * grad
-    first_hat = first_new / (1.0 - BETA_FIRST**STEP)
-    second_hat = second_new / (1.0 - BETA_SECOND**STEP)
-    weight_new = weight - rate * (
-        first_hat / (jnp.sqrt(second_hat) + ADAM_EPSILON) + DECAY_RATE * weight
-    )
-    return (first_new, second_new, weight_new)
-
-
-def adam_kernel(bo, tg, gs, sgrad, *refs):
-    small, mix_in, mix_out, gate_up, down = refs[0:5]
-    moments = refs[5:15]
-    bo_new, tg_new = refs[15:17]
-    outs = refs[17:]
-    bo_new[...] = bo[...]
-    tg_new[...] = tg[...]
-
-    def put(k, where, grad, weight, rate):
-        found = adam_step(weight[where], grad, moments[2 * k][where], moments[2 * k + 1][where], rate)
-        for ref, value in zip(outs[3 * k : 3 * k + 3], found):
-            ref[where] = value
-
-    put(0, ..., sgrad[...], small, RATE_SMALL)
-    for j in range(3):
-        put(1, j, gs[:, j * CH : (j + 1) * CH], mix_in, RATE_PROJ)
-    put(2, ..., gs[:, OUT_AT:GU_AT], mix_out, RATE_PROJ)
-    for i in range(TILES):
-        for j in range(2):
-            lo = GU_AT + (2 * i + j) * TILE
-            put(
-                3,
-                (j, slice(None), slice(i * TILE, (i + 1) * TILE)),
-                gs[:, lo : lo + TILE],
-                gate_up,
-                RATE_PROJ,
-            )
-    put(4, ..., gs[:, DOWN_AT:WIDE], down, RATE_DOWN)
+    )(lengths, tokens, cotangent, *state)
+
+
+def hand_over(*refs):
+    n = (len(refs) - 2) // 3
+    sources, targets, held = refs[:n], refs[n : 2 * n], refs[2 * n : 3 * n]
+    load_sem, store_sem = refs[3 * n :]
+    loads = [pltpu.make_async_copy(sources[i], held[i], load_sem.at[i]) for i in range(n)]
+    stores = [pltpu.make_async_copy(held[i], targets[i], store_sem.at[i]) for i in range(n)]
+    for c in loads:
+        c.start()
+    for i in range(n):
+        loads[i].wait()
+        stores[i].start()
+    for c in stores:
+        c.wait()
 
 
 def per_device(
@@ -757,14 +862,15 @@
     down_first,
     down_second,
 ):
-    place = ((lax.axis_index("dp") % 4) * 4 + lax.axis_index("tensor")) * 8
-    tile = lax.dynamic_update_slice(jnp.zeros((8, TILE), F32), small, (0, place))
-    bo, tg, gs, sg = train_call(
-        lengths, tokens, cotangent, tile, mix_in, mix_out, ffn_gate_up, ffn_down
-    )
-    sgrad = lax.dynamic_slice(sg, (0, place), small.shape)
-    weights = (small, mix_in, mix_out, ffn_gate_up, ffn_down)
-    moments = (
+    found = train_call(
+        lengths,
+        tokens,
+        cotangent,
+        small,
+        mix_in,
+        mix_out,
+        ffn_gate_up,
+        ffn_down,
         small_first,
         small_second,
         in_first,
@@ -776,18 +882,17 @@
         down_first,
         down_second,
     )
-    out_shape = [jax.ShapeDtypeStruct(v.shape, v.dtype) for v in (bo, tg)]
-    for v in weights:
-        out_shape += [jax.ShapeDtypeStruct(v.shape, v.dtype)] * 3
-    vmem = pl.BlockSpec(memory_space=pltpu.VMEM)
+    anywhere = pl.BlockSpec(memory_space=pltpu.HBM)
+    n = len(found)
     return tuple(
         pl.pallas_call(
-            adam_kernel,
-            out_shape=out_shape,
-            in_specs=[vmem] * 19,
-            out_specs=[vmem] * 17,
-            compiler_params=pltpu.CompilerParams(vmem_limit_bytes=32 * 1024 * 1024),
-        )(bo, tg, gs, sgrad, *weights, *moments)
+            hand_over,
+            out_shape=[jax.ShapeDtypeStruct(v.shape, v.dtype) for v in found],
+            in_specs=[anywhere] * n,
+            out_specs=[anywhere] * n,
+            scratch_shapes=[pltpu.VMEM(v.shape, v.dtype) for v in found]
+            + [pltpu.SemaphoreType.DMA((n,))] * 2,
+        )(*found)
     )
 
 

time: 175 us -> 146 us (0.83)
  Pallas kernels: 160 us -> 145 us
  local copies, waits for them, and re-layouts: 13.2 us -> 0 us
    pallas_call x2, Pallas kernels: 160 us -> 145 us  [the longest x1 142 us: train_call(): pl.pallas_call(train_kernel, out_shape=out_shape, in_specs=[pl.BlockSpec(...]
    unnamed x40 -> x0, local copies, waits for them, and re-layouts: 11.2 us -> none
where the time goes in v2:
time: 146 us
  Pallas kernels  145 us (99%)
    pallas_call x1, Pallas kernels, train_call(): pl.pallas_call(train_kernel, out_shape=out_shape, in_specs=[pl.BlockSpec(...  142 us

profile of v2, /device:TPU:0, one launch (start us, length us, event | category | flops | bytes accessed | tf_op | source)
XLA Modules:
  0.0 145.7 jit_solution(14320243473562660687)
XLA Ops:
  0.7 142.2 %shard_map.305 = (bf16[128,1024]{1,0:T(8,128)(2,1)}, f32[128,1024]{1,0:T(8,128)}, f32[5,8]{1,0:T(8,128)}, f32[5,8]{1,0:T(8,128)}, f32[5,8]{1,0:T(8,128)}, /*inde...) custom-call(s32[1,4]{1,0:T(1,128)} %refs_0_.1, ...), custom_call_target="tpu_custom_call" | custom-call | flops 14092861440 | bytes 8388608 | tf_op jit(solution)/shard_map/pallas_call | solution.py:771
  142.9 2.8 %shard_map.306 = (bf16[128,1024]{1,0:T(8,128)(2,1)}, f32[128,1024]{1,0:T(8,128)}, f32[5,8]{1,0:T(8,128)}, f32[5,8]{1,0:T(8,128)}, f32[5,8]{1,0:T(8,128)}, /*inde...) custom-call(bf16[128,1024]{1,0:T(8,128)(2,1)} %get-tuple-element.34., ...), custom_call_target="tpu_custom_call" | custom-call | tf_op jit(solution)/shard_map/pallas_call | solution.py:888

commit v3 on v2

--- a/solution.py
+++ b/solution.py
@@ -183,6 +183,9 @@
     to_core = (dp, ty * 2 + 1 - tc)
     to_far = (dp, (1 - ty) * 2 + tc)
     to_across = (dp, (1 - ty) * 2 + 1 - tc)
+    tensor_peers = (to_core, to_far, to_across)
+    x_peers = (to_xp, to_xo, to_xm)
+    z_peers = (to_zp, to_zo, to_zm)
     links = Links(send_sem, recv_sem)
 
     barrier = pltpu.get_barrier_semaphore()
@@ -228,6 +231,13 @@
         w[z, yh, x, :, j * CH : (j + 1) * CH] = state_in_w[0, j].astype(BF16)
     loads[2, 0].wait()
     w[z, yh, x, :, OUT_AT : OUT_AT + CH] = state_out_w[0].astype(BF16)
+    loads[3, 0].wait()
+    for i in range(TILES):
+        for j in range(2):
+            lo = GU_AT + (2 * i + j) * TILE
+            w[z, yh, x, :, lo : lo + TILE] = state_gu[0, j, :, i * TILE : (i + 1) * TILE].astype(BF16)
+    loads[4, 0].wait()
+    w[z, yh, x, :, DOWN_AT:WIDE] = state_down[0].astype(BF16)
     loads["tok"].wait()
     pl.semaphore_wait(barrier, len(peers))
 
@@ -245,6 +255,10 @@
     def w1a(p):
         a, b = w.at[z, :, x, lo_half, cols(p)], w.at[z, :, x, hi_half, cols(p)]
         return [same(a, to_xp), same(a, to_xm), same(b, to_zp), same(b, to_zm)]
+
+    def w1_all(p):
+        a, b = w.at[z, :, x, lo_half, cols(p)], w.at[z, :, x, hi_half, cols(p)]
+        return [same(a, to) for to in x_peers] + [same(b, to) for to in z_peers]
 
     def w1b(p):
         return [
@@ -277,33 +291,66 @@
     def rows_wait(copies):
         arrived(copies[1:])
 
+    def piece(i):
+        return pl.ds(i * (BLOCK // NZ), BLOCK // NZ)
+
+    class Pieces:
+        def __init__(self, ref):
+            self.ref, self.first = ref, links.take(3 * NZ)
+
+        def part(self, kind, i):
+            mine = self.ref.at[(1 - ty) if kind == 2 else ty, tc, piece(i)]
+            to = to_far if kind == 0 else to_core
+            return links.copy(mine, mine, to, self.first + kind * NZ + i)
+
+        def push(self, i):
+            self.part(0, i).start()
+            self.part(1, i).start()
+
+        def relay(self):
+            def step(i):
+                self.part(0, i).wait_recv()
+                self.part(2, i).start()
+
+            loop(NZ, step)
+
+        def wait(self):
+            for i in range(NZ):
+                self.part(1, i).wait_recv()
+                self.part(2, i).wait_recv()
+            links.open += [self.part(kind, i) for kind in range(3) for i in range(NZ)]
+
     def sum_start(u, lhs, lo, k):
-        first = links.take(NZ)
+        first, second = links.take(NZ), links.take(NZ)
+
+        def near(i):
+            return links.copy(ps.at[u, i], pr.at[u, i], to_core, first + i)
+
+        def far(i):
+            return links.copy(qs.at[u, i], qr.at[u, i], to_far, second + i)
 
         def step(i):
             wt = w[i, :, :, :, lo : lo + k].reshape(D // NZ, k)
             a = lhs[:, 1 - tc].reshape(2 * BLOCK, k)
             ps[u, i] = mm_nt(a, wt).astype(BF16).reshape(2, BLOCK, CH)
-            links.copy(ps.at[u, i], pr.at[u, i], to_core, first + i).start()
+            near(i).start()
             b = lhs[:, tc].reshape(2 * BLOCK, k)
             po[u, i] = mm_nt(b, wt).reshape(2, BLOCK, CH)
 
-        loop(NZ, step)
-        links.open += [links.copy(ps.at[u, i], pr.at[u, i], to_core, first + i) for i in range(NZ)]
-        return first
-
-    def sum_cross(u, first):
-        second = links.take(NZ)
-
-        def step(i):
-            links.copy(ps.at[u, i], pr.at[u, i], to_core, first + i).wait_recv()
+        def cross(i):
+            near(i).wait_recv()
             other = po[u, i, 1 - ty] + pr[u, i, 1 - ty].astype(F32)
             qs[u, i] = other.astype(BF16)
-            links.copy(qs.at[u, i], qr.at[u, i], to_far, second + i).start()
-            po[u, i, ty] = po[u, i, ty] + pr[u, i, ty].astype(F32)
-
-        loop(NZ, step)
-        links.open += [links.copy(qs.at[u, i], qr.at[u, i], to_far, second + i) for i in range(NZ)]
+            far(i).start()
+
+        def both(i):
+            step(i + 1)
+            cross(i)
+
+        step(0)
+        loop(NZ - 1, both)
+        cross(NZ - 1)
+        links.open += [near(i) for i in range(NZ)] + [far(i) for i in range(NZ)]
         return second
 
     def sum_wait(u, second):
@@ -312,7 +359,12 @@
 
     def sum_rows(u, lo, n):
         return jnp.concatenate(
-            [po[u, i, ty, pl.ds(lo, n), :] + qr[u, i, pl.ds(lo, n), :].astype(F32) for i in range(NZ)],
+            [
+                po[u, i, ty, pl.ds(lo, n), :]
+                + pr[u, i, ty, pl.ds(lo, n), :].astype(F32)
+                + qr[u, i, pl.ds(lo, n), :].astype(F32)
+                for i in range(NZ)
+            ],
             axis=1,
         )
 
@@ -374,6 +426,47 @@
             links.push(g.at[zo, 1, x, hi_half, c], r1s1.at[1, 1, :, c], to_zp),
         ]
 
+    def sum_second(p, copies):
+        c = cols(p)
+        arrived(copies)
+        loop(
+            8,
+            lambda i: add_two(
+                g.at[z, i // 4, i % 4, lo_half, c],
+                r2s2z.at[0, i // 4, i % 4, :, c],
+                r2s2z.at[1, i // 4, i % 4, :, c],
+            ),
+        )
+        loop(
+            8,
+            lambda i: add_two(
+                g.at[i // 2, i % 2, x, hi_half, c],
+                r2s2x.at[0, i // 2, i % 2, :, c],
+                r2s2x.at[1, i // 2, i % 2, :, c],
+            ),
+        )
+
+    def g1_all(p, copies):
+        c = cols(p)
+        sum_second(p, copies)
+        out = []
+        for i, (xx, to) in enumerate(((xp, to_xp), (xo, to_xo), (xm, to_xm))):
+            out.append(links.push(g.at[z, :, xx, lo_half, c], r1s2.at[0, i, :, :, c], to))
+        for i, (zz, to) in enumerate(((zp, to_zp), (zo, to_zo), (zm, to_zm))):
+            out.append(links.push(g.at[zz, :, x, hi_half, c], r1s2.at[1, i, :, :, c], to))
+        return out
+
+    def gy_all(p, copies):
+        c = cols(p)
+        arrived(copies)
+        for h, rows in enumerate((lo_half, hi_half)):
+            for y in range(2):
+                total = g[z, y, x, rows, c].astype(F32)
+                for i in range(3):
+                    total = total + r1s2[h, i, y, :, c].astype(F32)
+                g[z, y, x, rows, c] = total.astype(BF16)
+        return links.push(g.at[z, 1 - yh, x, :, c], ry.at[:, c], to_y)
+
     def g1b(p, copies):
         c = cols(p)
         out = []
@@ -440,9 +533,6 @@
             update(4, (), total(DOWN_AT, HID), RATE_DOWN)
             put(4)
 
-    tensor_peers = (to_core, to_far, to_across)
-    x_peers = (to_xp, to_xo, to_xm)
-    z_peers = (to_zp, to_zo, to_zm)
 
     def tile_send(src, slots, first, to_all):
         return [links.push(src, slots.at[first + i], to) for i, to in enumerate(to_all)]
@@ -453,41 +543,38 @@
 
     s_t = tile_send(st.at[0], sr, 0, tensor_peers)
     ya = wy(0)
-    tok_c = rows_start(tok)
-    loads[3, 0].wait()
-    for i in range(TILES):
-        for j in range(2):
-            lo = GU_AT + (2 * i + j) * TILE
-            w[z, yh, x, :, lo : lo + TILE] = state_gu[0, j, :, i * TILE : (i + 1) * TILE].astype(BF16)
     yb = wy(1)
     ye = wy(2)
-    loads[4, 0].wait()
-    w[z, yh, x, :, DOWN_AT:WIDE] = state_down[0].astype(BF16)
     yc = wy(3)
+    tok_c = rows_start(tok)
     st[1] = tile_sum(st[0], sr, 0, s_t)
     s_x = tile_send(st.at[1], sr, 3, x_peers)
     ya.wait_recv()
-    a1 = w1a(0)
+    a1 = w1_all(0)
     sm[z, yh] = tile_sum(st[1], sr, 3, s_x)
     s_y = same(sm.at[z, yh], to_y)
-    arrived(a1)
-    a1 = w1b(0)
     yb.wait_recv()
     b1 = w1a(1)
+    arrived(a1)
+    a2 = w2a(0)
     s_y.wait_recv()
     s_z = [same(sm.at[z], to) for to in z_peers]
-    arrived(a1)
-    a2 = w2a(0)
-    rows_relay(tok, tok_c)
     ye.wait_recv()
     e1 = w1a(2)
     arrived(b1)
     b1 = w1b(1)
     yc.wait_recv()
     c1 = w1a(3)
+    arrived(e1)
+    e1 = w1b(2)
+    rows_relay(tok, tok_c)
     arrived(s_z)
     for k in range(8):
         sml[:, k * TILE : (k + 1) * TILE] = sm[k // 2, k % 2]
+    arrived(b1)
+    arrived(a2)
+    a2 = w2b(0)
+    b2 = w2a(1)
     rows_wait(tok_c)
 
     def norm_in(i):
@@ -498,12 +585,6 @@
         invs[a, b, pl.ds(r, 32), :] = jnp.broadcast_to(inv, (32, TILE))
 
     loop(16, norm_in)
-    arrived(e1)
-    e1 = w1b(2)
-    arrived(b1)
-    arrived(a2)
-    a2 = w2b(0)
-    b2 = w2a(1)
     arrived(c1)
     c1 = w1b(3)
     loads["cot"].wait()
@@ -535,12 +616,11 @@
         conv[:, lanes] = v
         gated[:, :, :, lanes] = (pj[1, :, lanes] * v).astype(BF16).reshape(2, 2, BLOCK, TILE)
 
-    m_first = sum_start(0, gated, OUT_AT, CH)
+    m_second = sum_start(0, gated, OUT_AT, CH)
     arrived(b2)
     b2 = w2b(1)
     arrived(e1)
     e2 = w2a(2)
-    m_second = sum_cross(0, m_first)
     sum_wait(0, m_second)
 
     def norm_mid(i):
@@ -549,16 +629,17 @@
         mid[pl.ds(r, 32), :] = v
         inv = lax.rsqrt(jnp.mean(v * v, axis=1, keepdims=True) + NORM_EPSILON)
         two[ty, tc, pl.ds(r, 32), :] = (v * inv * sml[1:2, :]).astype(BF16)
-
+        two_c.push(i)
+
+    two_c = Pieces(two)
     loop(4, norm_mid)
-    two_c = rows_start(two)
     rows_relay(cot, cot_c)
     arrived(e2)
     e2 = w2b(2)
     arrived(c1)
     c2 = w2a(3)
-    rows_relay(two, two_c)
-    rows_wait(two_c)
+    two_c.relay()
+    two_c.wait()
     arrived(b2)
 
     def gate_up(i):
@@ -619,14 +700,9 @@
         mm(cot[...].reshape(ROWS, D), w[:, :, :, :, WIDE - TILE : WIDE].reshape(D, TILE)),
     )
     gc_ = g2b(3, gc_)
+    n_second = sum_start(1, gg, GU_AT, 2 * HID)
     gate_up_grad(1)
     gb_ = g2a(1)
-    n_first = sum_start(1, gg, GU_AT, 2 * HID)
-    gate_up_grad(2)
-    ge_ = g2a(2)
-    n_second = sum_cross(1, n_first)
-    gc_ = g1a(3, gc_)
-    gb_ = g2b(1, gb_)
     sum_wait(1, n_second)
     gacc[...] = jnp.zeros_like(gacc)
 
@@ -642,15 +718,16 @@
         out = cot[ty, tc, pl.ds(r, 32), :].astype(F32) + inv * (scaled - unit * inner)
         gmid[pl.ds(r, 32), :] = out
         rmid[ty, tc, pl.ds(r, 32), :] = out.astype(BF16)
-
+        mid_c.push(i)
+
+    mid_c = Pieces(rmid)
     loop(4, norm_two_back)
-    mid_c = rows_start(rmid)
-    o_first = sum_start(2, hid, DOWN_AT, HID)
-    ge_ = g2b(2, ge_)
-    gc_ = g1b(3, gc_)
-    rows_relay(rmid, mid_c)
-    o_second = sum_cross(2, o_first)
-    rows_wait(mid_c)
+    gate_up_grad(2)
+    ge_ = g2a(2)
+    gc_ = g1a(3, gc_)
+    mid_c.relay()
+    gb_ = g2b(1, gb_)
+    mid_c.wait()
 
     pg = mm(rmid[...].reshape(ROWS, D), w[:, :, :, :, OUT_AT : OUT_AT + CH].reshape(D, CH))
     for q in range(2):
@@ -674,7 +751,7 @@
             lo = j * CH + q * TILE
             gp[:, :, :, lo : lo + TILE] = v.astype(BF16).reshape(2, 2, BLOCK, TILE)
 
-    i_first = sum_start(3, gp, 0, 3 * CH)
+    i_second = sum_start(3, gp, 0, 3 * CH)
 
     def mix_grad(i):
         a = one[:, :, :, at_lane(i, CH)].reshape(ROWS, CH).T
@@ -701,31 +778,12 @@
         links.push(sgr.at[zz], gr.at[i], to)
         for i, (zz, to) in enumerate(((zp, to_zp), (zo, to_zo), (zm, to_zm)))
     ]
-    i_second = sum_cross(3, i_first)
+    ge_ = g2b(2, ge_)
     gb_ = g1a(1, gb_)
-    gc_ = gy(3, gc_)
+    gc_ = g1b(3, gc_)
     arrived(u_z)
     sgr[z] = sgr[z] + gr[0] + gr[1] + gr[2]
     u_y = links.push(sgr.at[z, 1 - yh], gc.at[0], to_y)
-    ge_ = g1a(2, ge_)
-    ga_ = g2b(0, ga_)
-    gb_ = g1b(1, gb_)
-    u_y.wait_recv()
-    gc[1] = sgr[z, yh] + gc[0]
-    u_x = tile_send(gc.at[1], gc, 2, x_peers)
-    sum_wait(2, o_second)
-
-    def out_rows(i):
-        r = i * 32
-        bo[pl.ds(r, 32), :] = (mid[pl.ds(r, 32), :] + sum_rows(2, r, 32)).astype(BF16)
-
-    loop(4, out_rows)
-    store(bo, bo_out)
-    ge_ = g1b(2, ge_)
-    gb_ = gy(1, gb_)
-    gend(3, gc_)
-    gc[5] = tile_sum(gc[1], gc, 2, u_x)
-    u_t = tile_send(gc.at[5], gc, 6, tensor_peers)
     sum_wait(3, i_second)
 
     def norm_one_back(i):
@@ -740,17 +798,37 @@
 
     loop(4, norm_one_back)
     store(tg, tg_out)
+    ga_ = g2b(0, ga_)
+    gb_ = g1b(1, gb_)
+    u_y.wait_recv()
+    gc[1] = sgr[z, yh] + gc[0]
+    u_x = tile_send(gc.at[1], gc, 2, x_peers)
+    o_second = sum_start(2, hid, DOWN_AT, HID)
+    ge_ = g1a(2, ge_)
+    gc_ = gy(3, gc_)
+    gc[5] = tile_sum(gc[1], gc, 2, u_x)
+    u_t = tile_send(gc.at[5], gc, 6, tensor_peers)
+    ga_ = g1_all(0, ga_)
+    gb_ = gy(1, gb_)
+    ge_ = g1b(2, ge_)
+    sum_wait(2, o_second)
+
+    def out_rows(i):
+        r = i * 32
+        bo[pl.ds(r, 32), :] = (mid[pl.ds(r, 32), :] + sum_rows(2, r, 32)).astype(BF16)
+
+    loop(4, out_rows)
+    store(bo, bo_out)
+    gend(3, gc_)
+    ga_ = gy_all(0, ga_)
     ge_ = gy(2, ge_)
     gend(1, gb_)
-    ga_ = g1a(0, ga_)
     gc[9] = pltpu.roll(tile_sum(gc[5], gc, 6, u_t), TILE - place, 1)
     for j in (1, 2):
         loads[0, j].wait()
     update(0, (), gc[9, 0:5, 0:8], RATE_SMALL)
     put(0)
     gend(2, ge_)
-    ga_ = g1b(0, ga_)
-    ga_ = gy(0, ga_)
     gend(0, ga_)
     for c in links.open:
         c.wait_send()
@@ -758,7 +836,7 @@
         c.wait()
 
 
-N_COPIES = 220
+N_COPIES = 240
 
 
 def train_call(lengths, tokens, cotangent, *state):
@@ -813,7 +891,7 @@
             pltpu.VMEM((2, NY, NX, HALF, WIDE), BF16),
             pltpu.VMEM((2, NZ, NY, HALF, WIDE), BF16),
             pltpu.VMEM((2, 2, HALF, WIDE), BF16),
-            pltpu.VMEM((2, 2, 2, HALF, WIDE), BF16),
+            pltpu.VMEM((2, 3, 2, HALF, WIDE), BF16),
             pltpu.VMEM((SHARD, WIDE), BF16),
             pltpu.SemaphoreType.DMA((N_COPIES,)),
             pltpu.SemaphoreType.DMA((N_COPIES,)),

time: 146 us -> 140 us (0.959)
  Pallas kernels: 145 us -> 139 us
    pallas_call x1, Pallas kernels: 142 us -> 136 us  [train_call(): pl.pallas_call(train_kernel, out_shape=out_shape, in_specs=[pl.BlockSpec(...]
where the time goes in v3:
time: 140 us
  Pallas kernels  139 us (99%)
    pallas_call x1, Pallas kernels, train_call(): pl.pallas_call(train_kernel, out_shape=out_shape, in_specs=[pl.BlockSpec(...  136 us
    pallas_call x1, Pallas kernels, per_device(): pl.pallas_call(hand_over, out_shape=[jax.ShapeDtypeStruct(v.shape, v.dtyp...  2.82 us

profile of v3, /device:TPU:0, one launch (start us, length us, event | category | flops | bytes accessed | tf_op | source)
XLA Modules:
  0.0 139.9 jit_solution(7293470078373139761)
XLA Ops:
  0.7 136.4 %shard_map.305 = (bf16[128,1024]{1,0:T(8,128)(2,1)}, f32[128,1024]{1,0:T(8,128)}, f32[5,8]{1,0:T(8,128)}, f32[5,8]{1,0:T(8,128)}, f32[5,8]{1,0:T(8,128)}, /*inde...) custom-call(s32[1,4]{1,0:T(1,128)} %refs_0_.1, ...), custom_call_target="tpu_custom_call" | custom-call | flops 14092861440 | bytes 8388608 | tf_op jit(solution)/shard_map/pallas_call | solution.py:849
  137.1 2.8 %shard_map.306 = (bf16[128,1024]{1,0:T(8,128)(2,1)}, f32[128,1024]{1,0:T(8,128)}, f32[5,8]{1,0:T(8,128)}, f32[5,8]{1,0:T(8,128)}, f32[5,8]{1,0:T(8,128)}, /*inde...) custom-call(bf16[128,1024]{1,0:T(8,128)(2,1)} %get-tuple-element.34., ...), custom_call_target="tpu_custom_call" | custom-call | tf_op jit(solution)/shard_map/pallas_call | solution.py:966

commit v4 on v3

--- a/solution.py
+++ b/solution.py
@@ -616,11 +616,11 @@
         conv[:, lanes] = v
         gated[:, :, :, lanes] = (pj[1, :, lanes] * v).astype(BF16).reshape(2, 2, BLOCK, TILE)
 
-    m_second = sum_start(0, gated, OUT_AT, CH)
     arrived(b2)
     b2 = w2b(1)
     arrived(e1)
     e2 = w2a(2)
+    m_second = sum_start(0, gated, OUT_AT, CH)
     sum_wait(0, m_second)
 
     def norm_mid(i):
@@ -722,11 +722,12 @@
 
     mid_c = Pieces(rmid)
     loop(4, norm_two_back)
+    gb_ = g2b(1, gb_)
     gate_up_grad(2)
     ge_ = g2a(2)
     gc_ = g1a(3, gc_)
     mid_c.relay()
-    gb_ = g2b(1, gb_)
+    ge_ = g2b(2, ge_)
     mid_c.wait()
 
     pg = mm(rmid[...].reshape(ROWS, D), w[:, :, :, :, OUT_AT : OUT_AT + CH].reshape(D, CH))
@@ -778,12 +779,18 @@
         links.push(sgr.at[zz], gr.at[i], to)
         for i, (zz, to) in enumerate(((zp, to_zp), (zo, to_zo), (zm, to_zm)))
     ]
-    ge_ = g2b(2, ge_)
     gb_ = g1a(1, gb_)
     gc_ = g1b(3, gc_)
+    ga_ = g2b(0, ga_)
     arrived(u_z)
     sgr[z] = sgr[z] + gr[0] + gr[1] + gr[2]
     u_y = links.push(sgr.at[z, 1 - yh], gc.at[0], to_y)
+    o_second = sum_start(2, hid, DOWN_AT, HID)
+    ge_ = g1a(2, ge_)
+    gb_ = g1b(1, gb_)
+    u_y.wait_recv()
+    gc[1] = sgr[z, yh] + gc[0]
+    u_x = tile_send(gc.at[1], gc, 2, x_peers)
     sum_wait(3, i_second)
 
     def norm_one_back(i):
@@ -798,19 +805,12 @@
 
     loop(4, norm_one_back)
     store(tg, tg_out)
-    ga_ = g2b(0, ga_)
-    gb_ = g1b(1, gb_)
-    u_y.wait_recv()
-    gc[1] = sgr[z, yh] + gc[0]
-    u_x = tile_send(gc.at[1], gc, 2, x_peers)
-    o_second = sum_start(2, hid, DOWN_AT, HID)
-    ge_ = g1a(2, ge_)
+    ga_ = g1_all(0, ga_)
     gc_ = gy(3, gc_)
+    ge_ = g1b(2, ge_)
     gc[5] = tile_sum(gc[1], gc, 2, u_x)
     u_t = tile_send(gc.at[5], gc, 6, tensor_peers)
-    ga_ = g1_all(0, ga_)
     gb_ = gy(1, gb_)
-    ge_ = g1b(2, ge_)
     sum_wait(2, o_second)
 
     def out_rows(i):
@@ -819,8 +819,8 @@
 
     loop(4, out_rows)
     store(bo, bo_out)
+    ga_ = gy_all(0, ga_)
     gend(3, gc_)
-    ga_ = gy_all(0, ga_)
     ge_ = gy(2, ge_)
     gend(1, gb_)
     gc[9] = pltpu.roll(tile_sum(gc[5], gc, 6, u_t), TILE - place, 1)

time: 140 us -> 139 us (level)
    pallas_call x1, Pallas kernels: 136 us -> 135 us  [train_call(): pl.pallas_call(train_kernel, out_shape=out_shape, in_specs=[pl.BlockSpec(...]
where the time goes in v4:
time: 139 us
  Pallas kernels  138 us (99%)
    pallas_call x1, Pallas kernels, train_call(): pl.pallas_call(train_kernel, out_shape=out_shape, in_specs=[pl.BlockSpec(...  135 us
    pallas_call x1, Pallas kernels, per_device(): pl.pallas_call(hand_over, out_shape=[jax.ShapeDtypeStruct(v.shape, v.dtyp...  2.82 us

profile of v4, /device:TPU:0, one launch (start us, length us, event | category | flops | bytes accessed | tf_op | source)
XLA Modules:
  0.0 138.5 jit_solution(5373268943932663481)
XLA Ops:
  0.7 135.0 %shard_map.305 = (bf16[128,1024]{1,0:T(8,128)(2,1)}, f32[128,1024]{1,0:T(8,128)}, f32[5,8]{1,0:T(8,128)}, f32[5,8]{1,0:T(8,128)}, f32[5,8]{1,0:T(8,128)}, /*inde...) custom-call(s32[1,4]{1,0:T(1,128)} %refs_0_.1, ...), custom_call_target="tpu_custom_call" | custom-call | flops 14092861440 | bytes 8388608 | tf_op jit(solution)/shard_map/pallas_call | solution.py:849
  135.7 2.8 %shard_map.306 = (bf16[128,1024]{1,0:T(8,128)(2,1)}, f32[128,1024]{1,0:T(8,128)}, f32[5,8]{1,0:T(8,128)}, f32[5,8]{1,0:T(8,128)}, f32[5,8]{1,0:T(8,128)}, /*inde...) custom-call(bf16[128,1024]{1,0:T(8,128)(2,1)} %get-tuple-element.34., ...), custom_call_target="tpu_custom_call" | custom-call | tf_op jit(solution)/shard_map/pallas_call | solution.py:966
